TPU v7x, 512 devices: a whole 4x8x8 slice. The times are simulated.
512 devices in a mesh: slab: 32 (over y, x), band: 16 (over z, core).
Axes of the slice: x: 4, y: 8, z: 8, core: 2. Of those that a mesh axis runs over, the one named last changes fastest.
Arguments:
- projections: bfloat16 [4096, 18, 512], P('band', None, 'slab'), may hold values from -0.09375 to 0.09375
- occupation: float32 [4096], P('band'), may hold values from 0.5 to 2
- augment_tables: bfloat16 [2, 171, 48, 2304], P(None, None, 'band'), may hold values from -0.01953125 to 0.01953125
- box_root: int32 [512], P('slab'), may hold values from 0 to 575, as said below
- box_xy: int32 [512], P('slab'), may hold values from 0 to 2303
- species: int32 [512], P('slab'), may hold values from 0 to 1
- potential: float32 [576, 2304], P('slab'), may hold values from -6 to 6
Outputs:
- aug_density: float32 [576, 2304], P('slab')
- integrals: float32 [171, 512], P(None, ('slab', 'band'))
Inputs may be any that keep to these rules, and one draw needn't show every extreme that they name: `box_root`: atom a's root lies in the planes of the slab that stores it, from (a // 16) * 18 to (a // 16) * 18 + 17; in every slab some atom starts at the slab's first plane and some at its last.
All inputs are finite; a program needn't handle non-finite values.
Results may differ from a plain program's by a relative error of at most 0.0031.
Values may be sent and summed in bfloat16 or wider, within the bound.
A program may use at most 64 MiB of HBM per device.

v0:
```python
import jax
import jax.numpy as jnp
import numpy as np
from jax import lax
from jax.sharding import PartitionSpec as P

GX = 48


def shifted(block, axis, distance):
    devices = range(lax.axis_size(axis))
    route = [((i - distance) % len(devices), i) for i in devices]
    return lax.ppermute(block, axis, route)


def shift_tables(anchor, side, dtype):
    line = jnp.arange(side, dtype=jnp.int32)
    row_target = (anchor[:, None] // side + line[None, :]) % side
    col_target = (anchor[:, None] % side + line[None, :]) % side
    row_onehot = (line[None, :, None] == row_target[:, None, :]).astype(dtype)
    col_onehot = (line[None, :, None] == col_target[:, None, :]).astype(dtype)
    return (row_onehot, col_onehot)


def shards(projections, occupation, augment_tables, box_root, box_xy, species, potential):
    proj_count = projections.shape[1]
    slab_atoms = projections.shape[2]
    groups = lax.axis_size("band")
    member = lax.axis_index("band")
    slab_index = lax.axis_index("slab")
    species_count, pair_count, my_depth, columns = augment_tables.shape
    box_depth = my_depth * groups
    planes = potential.shape[0]
    blocks = (planes + box_depth - 2) // planes + 1
    owned_atoms = slab_atoms // groups
    row_index, col_index = np.triu_indices(proj_count)
    factor = np.where(row_index == col_index, 1.0, 2.0).astype(np.float32)
    weighted = projections.astype(jnp.float32) * occupation[:, None, None]
    outer_sums = jnp.einsum(
        "nia,nja->ija", weighted, projections.astype(jnp.float32), precision=lax.Precision.HIGHEST
    )
    partial_sum = outer_sums[row_index, col_index] * jnp.asarray(factor)[:, None]
    band_total = lax.psum(partial_sum, "band")
    packed = band_total.astype(jnp.bfloat16)
    offsets = box_root - slab_index * planes + member * my_depth
    masked = [
        jnp.where(species[None, :] == species_id, packed, jnp.zeros_like(packed))
        for species_id in range(species_count)
    ]
    stacked = jnp.concatenate(masked, axis=0)
    flat_tables = augment_tables.reshape(species_count * pair_count, my_depth * columns)
    box_terms = lax.dot_general(
        stacked, flat_tables, (((0,), (0,)), ((), ())), preferred_element_type=jnp.float32
    )
    box_terms = box_terms.reshape(slab_atoms, my_depth, GX, GX)
    row_exact, col_exact = shift_tables(box_xy, GX, jnp.float32)
    moved_rows = jnp.einsum("aRr,adrc->adRc", row_exact, box_terms, precision=lax.Precision.HIGHEST)
    placed = jnp.einsum("aCc,adRc->adRC", col_exact, moved_rows, precision=lax.Precision.HIGHEST)
    box_rows = placed.reshape(slab_atoms * my_depth, columns)
    plane_ids = (offsets[:, None] + jnp.arange(my_depth, dtype=jnp.int32)[None, :]).reshape(-1)
    plane_line = jnp.arange(blocks * planes, dtype=jnp.int32)
    plane_onehot = plane_line[:, None] == plane_ids[None, :]
    extended = jnp.dot(
        plane_onehot.astype(jnp.float32),
        box_rows,
        precision=lax.Precision.HIGHEST,
        preferred_element_type=jnp.float32,
    )
    summed = lax.psum(extended, "band")
    density = summed[:planes]
    for offset_block in range(1, blocks):
        density = density + shifted(
            summed[offset_block * planes : (offset_block + 1) * planes], "slab", offset_block
        )
    rounded = potential.astype(jnp.bfloat16)
    stacked_planes = [rounded]
    for offset_block in range(1, blocks):
        stacked_planes.append(shifted(rounded, "slab", -offset_block))
    window = jnp.concatenate(stacked_planes, axis=0)
    picked = jnp.dot(
        plane_onehot.T.astype(jnp.bfloat16), window, preferred_element_type=jnp.float32
    ).astype(jnp.bfloat16)
    picked = picked.reshape(slab_atoms, my_depth, GX, GX)
    row_select, col_select = shift_tables(box_xy, GX, jnp.bfloat16)
    rows_back = jnp.einsum(
        "aRr,adRC->adrC", row_select, picked, preferred_element_type=jnp.float32
    ).astype(jnp.bfloat16)
    box_values = jnp.einsum(
        "aCc,adrC->adrc", col_select, rows_back, preferred_element_type=jnp.float32
    ).astype(jnp.bfloat16)
    box_values = box_values.reshape(slab_atoms, my_depth * columns)
    projected = lax.dot_general(
        flat_tables, box_values, (((1,), (1,)), ((), ())), preferred_element_type=jnp.float32
    )
    partial_ints = jnp.zeros((pair_count, slab_atoms), jnp.float32)
    for species_id in range(species_count):
        piece = projected[species_id * pair_count : (species_id + 1) * pair_count]
        partial_ints = partial_ints + jnp.where(
            species[None, :] == species_id, piece, jnp.zeros_like(piece)
        )
    total_ints = lax.psum(partial_ints, "band")
    integrals = lax.dynamic_slice_in_dim(total_ints, member * owned_atoms, owned_atoms, 1)
    return (density, integrals)


def solution(mesh):
    placed = (
        P("band", None, "slab"),
        P("band"),
        P(None, None, "band", None),
        P("slab"),
        P("slab"),
        P("slab"),
        P("slab", None),
    )
    return jax.shard_map(
        shards,
        mesh=mesh,
        in_specs=placed,
        out_specs=(P("slab", None), P(None, ("slab", "band"))),
        check_vma=False,
    )
```

profile of v0, /device:TPU:1, one launch (start us, length us, event | category | flops | bytes accessed | tf_op | source)
XLA Modules:
  0.0 260.4 jit_solution(18213536691788302659)
XLA Ops:
  7.2 0.9 convert_element_type.30
  8.2 6.9 %collective-permute-start.5 = (bf16[18,2304]{1,0:T(8,128)(2,1)S(1)}, bf16[18,2304]{1,0:T(8,128)(2,1)S(1)}, u32[]{:S(2)}, u32[]{:S(2)}) collective-permute-start(bf16[18,2304]{1,0:T(8,128)(2,1)S(1)} %convert_element_type.30), channel_id=1, source_target_pairs={{48,0},{64,16},{80,32},{96,48},{112,64},{128,80},{144,96},{160,112... | collective-permute-start | bytes 248840 | tf_op jit(solution)/shard_map/ppermute | solution.py:13
  15.0 5.1 %collective-permute-start.4 = (bf16[18,2304]{1,0:T(8,128)(2,1)S(1)}, bf16[18,2304]{1,0:T(8,128)(2,1)S(1)}, u32[]{:S(2)}, u32[]{:S(2)}) collective-permute-start(bf16[18,2304]{1,0:T(8,128)(2,1)S(1)} %convert_element_type.30), channel_id=1, source_target_pairs={{32,0},{48,16},{64,32},{80,48},{96,64},{112,80},{128,96},{144,112}... | collective-permute-start | bytes 248840 | tf_op jit(solution)/shard_map/ppermute | solution.py:13
  20.2 3.1 %collective-permute-start.3 = (bf16[18,2304]{1,0:T(8,128)(2,1)S(1)}, bf16[18,2304]{1,0:T(8,128)(2,1)}, u32[]{:S(2)}, u32[]{:S(2)}) collective-permute-start(bf16[18,2304]{1,0:T(8,128)(2,1)S(1)} %convert_element_type.30), channel_id=1, source_target_pairs={{16,0},{32,16},{48,32},{64,48},{80,64},{96,80},{112,96},{128,112},... | collective-permute-start | bytes 248840 | tf_op jit(solution)/shard_map/ppermute | solution.py:13
  24.3 1.4 convolution_bitcast_fusion.1
  25.9 2.1 gather_fusion
  28.3 7.4 %copy.22 = bf16[2,171,3,2304]{3,2,1,0:T(4,128)(2,1)} copy(bf16[2,171,3,2304]{3,0,2,1:T(2,128)(2,1)} %param.14) | data formatting | bytes 9455616 | tf_op args[2]
  35.7 5.2 %pad.6 = bf16[344,3,2304]{2,1,0:T(4,128)(2,1)S(1)} pad(bf16[342,3,2304]{2,1,0:T(4,128)(2,1)} %bitcast.48, bf16[]{:T(256)} %constant.65.clone.1), padding=0_2x0_0x0_0 | pad | bytes 9483266
  40.9 3.0 %copy.28 = bf16[43,8,3,2304]{3,1,2,0:T(8,128)(2,1)} copy(bf16[43,8,3,2304]{3,2,1,0:T(4,128)(2,1)S(1)} %bitcast.47) | data formatting | bytes 9510912
  43.9 7.8 %copy.23 = bf16[6912,342]{1,0:T(8,128)(2,1)} copy(bf16[6912,342]{0,1:T(8,128)(2,1)} %bitcast.45) | data formatting | bytes 9455616 | tf_op jit(solution)/shard_map/dot_general | solution.py:52
  51.9 1.2 convolution_convert_fusion
  55.1 3.7 %convolution_bitcast_fusion.2 = f32[342,16]{0,1:T(8,128)S(1)} fusion(bf16[16,6912]{1,0:T(8,128)(2,1)S(1)} %reshape.102, bf16[342,6912]{1,0:T(8,128)(2,1)} %bitcast.46), kind=kOutput, calls=%fused_computation.8 | convolution fusion | flops 75644928 | bytes 4970880 | tf_op jit(solution)/shard_map/dot_general | solution.py:92
  58.9 51.2 %all-reduce = (bf16[171,16]{0,1:T(8,128)(2,1)S(1)}, f32[171,16]{0,1:T(8,128)S(1)}) all-reduce(f32[171,16]{0,1:T(8,128)S(1)} %broadcast_multiply_fusion, f32[171,16]{0,1:T(8,128)S(1)} %fusion.29), channel_id=1, replica_groups=mesh['slab'=32,'band'=16] {'band'}, use_global_device_ids=true, to_apply=%region_0.0 | all-reduce | flops 5472 | bytes 38304 | tf_op jit(solution)/shard_map/psum | solution.py:43
  110.1 6.0 %fusion.30 = f32[16,3,48,48]{3,0,2,1:T(8,128)S(1)} fusion(bf16[3,48,48,342]{3,2,1,0:T(8,128)(2,1)} %bitcast.49, bf16[171,16]{0,1:T(8,128)(2,1)S(1)} %get-tuple-element.8, bf16[171,16]{0,1:T(8,128)(2,1)S(1)} %get-tuple-element.7), kind=kOutput, calls=%fused_computation.39 | convolution fusion | flops 75666816 | bytes 5181120 | tf_op jit(solution)/shard_map/dot_general | solution.py:52
  116.1 1.1 convolution_bitcast_fusion
  118.5 1.3 fusion.26
  119.8 109.1 %all-reduce.3.cloned.1.call-done = f32[72,2304]{1,0:T(8,128)} async-done(((f32[72,2304]{1,0:T(8,128)}), f32[72,2304]{1,0:T(8,128)}) %all-reduce.3.cloned.1.call-update) | async-done | bytes 663568 | tf_op jit(solution)/shard_map/psum | solution.py:69
  228.9 1.2 fusion.41
  230.2 4.3 %collective-permute-start.2 = (f32[18,2304]{1,0:T(8,128)S(1)}, f32[18,2304]{1,0:T(8,128)S(1)}, u32[]{:S(2)}, u32[]{:S(2)}) collective-permute-start(f32[18,2304]{1,0:T(8,128)S(1)} %get-tuple-element.5), channel_id=1, source_target_pairs={{464,0},{480,16},{496,32},{0,48},{16,64},{32,80},{48,96},{64,112},... | collective-permute-start | bytes 497672 | tf_op jit(solution)/shard_map/ppermute | solution.py:13
  234.5 3.4 %collective-permute-start.1 = (f32[18,2304]{1,0:T(8,128)S(1)}, f32[18,2304]{1,0:T(8,128)S(1)}, u32[]{:S(2)}, u32[]{:S(2)}) collective-permute-start(f32[18,2304]{1,0:T(8,128)S(1)} %get-tuple-element.6), channel_id=1, source_target_pairs={{480,0},{496,16},{0,32},{16,48},{32,64},{48,80},{64,96},{80,112},{... | collective-permute-start | bytes 497672 | tf_op jit(solution)/shard_map/ppermute | solution.py:13
  237.9 2.5 collective-permute-start
  241.0 6.3 %collective-permute-done.1 = f32[18,2304]{1,0:T(8,128)S(1)} collective-permute-done((f32[18,2304]{1,0:T(8,128)S(1)}, f32[18,2304]{1,0:T(8,128)S(1)}, u32[]{:S(2)}, u32[]{:S(2)}) %collective-permute-start.1) | collective-permute-done | bytes 165920 | tf_op jit(solution)/shard_map/ppermute | solution.py:13
  247.2 4.6 %collective-permute-done = f32[18,2304]{1,0:T(8,128)S(1)} collective-permute-done((f32[18,2304]{1,0:T(8,128)S(1)}, f32[18,2304]{1,0:T(8,128)S(1)}, u32[]{:S(2)}, u32[]{:S(2)}) %collective-permute-start) | collective-permute-done | bytes 165920 | tf_op jit(solution)/shard_map/ppermute | solution.py:13
  251.9 1.7 fusion.19
  (34 shorter events, 5.6 us)
Async XLA Ops:
  7.2 18.7 %copy-start = (s32[171]{0:T(256)S(1)}, s32[171]{0:T(256)}, u32[]{:S(2)}) copy-start(s32[171]{0:T(256)} %constant.104) | copy-start | bytes 2056
  7.2 221.8 %all-reduce.3.cloned.1.call-start = ((), (), s32[]{:S(2)}) async-start(), calls=%async_computation | async-start | bytes 1327104 | tf_op jit(solution)/shard_map/psum | solution.py:69
  8.2 43.7 %collective-permute-start.5 = (bf16[18,2304]{1,0:T(8,128)(2,1)S(1)}, bf16[18,2304]{1,0:T(8,128)(2,1)S(1)}, u32[]{:S(2)}, u32[]{:S(2)}) collective-permute-start(bf16[18,2304]{1,0:T(8,128)(2,1)S(1)} %convert_element_type.30), channel_id=1, source_target_pairs={{48,0},{64,16},{80,32},{96,48},{112,64},{128,80},{144,96},{160,112... | collective-permute-start | bytes 248840 | tf_op jit(solution)/shard_map/ppermute | solution.py:13
  15.0 36.8 %collective-permute-start.4 = (bf16[18,2304]{1,0:T(8,128)(2,1)S(1)}, bf16[18,2304]{1,0:T(8,128)(2,1)S(1)}, u32[]{:S(2)}, u32[]{:S(2)}) collective-permute-start(bf16[18,2304]{1,0:T(8,128)(2,1)S(1)} %convert_element_type.30), channel_id=1, source_target_pairs={{32,0},{48,16},{64,32},{80,48},{96,64},{112,80},{128,96},{144,112}... | collective-permute-start | bytes 248840 | tf_op jit(solution)/shard_map/ppermute | solution.py:13
  20.2 31.7 %collective-permute-start.3 = (bf16[18,2304]{1,0:T(8,128)(2,1)S(1)}, bf16[18,2304]{1,0:T(8,128)(2,1)}, u32[]{:S(2)}, u32[]{:S(2)}) collective-permute-start(bf16[18,2304]{1,0:T(8,128)(2,1)S(1)} %convert_element_type.30), channel_id=1, source_target_pairs={{16,0},{32,16},{48,32},{64,48},{80,64},{96,80},{112,96},{128,112},... | collective-permute-start | bytes 248840 | tf_op jit(solution)/shard_map/ppermute | solution.py:13
  24.2 3.8 %copy-start.2 = (s32[16]{0:T(128)S(1)}, s32[16]{0:T(128)}, u32[]{:S(2)}) copy-start(s32[16]{0:T(128)} %param.15) | copy-start | bytes 196
  24.2 3.9 %copy-start.3 = (s32[16]{0:T(128)S(1)}, s32[16]{0:T(128)}, u32[]{:S(2)}) copy-start(s32[16]{0:T(128)} %param.16) | copy-start | bytes 196
  24.2 3.9 %copy-start.1 = (f32[171]{0:T(256)S(1)}, f32[171]{0:T(256)}, u32[]{:S(2)}) copy-start(f32[171]{0:T(256)} %constant.74.clone) | copy-start | bytes 2056
  24.2 4.0 %copy-start.4 = (s32[16]{0:T(128)S(1)}, s32[16]{0:T(128)}, u32[]{:S(2)}) copy-start(s32[16]{0:T(128)} %param.17) | copy-start | bytes 196
  230.2 10.8 %collective-permute-start.2 = (f32[18,2304]{1,0:T(8,128)S(1)}, f32[18,2304]{1,0:T(8,128)S(1)}, u32[]{:S(2)}, u32[]{:S(2)}) collective-permute-start(f32[18,2304]{1,0:T(8,128)S(1)} %get-tuple-element.5), channel_id=1, source_target_pairs={{464,0},{480,16},{496,32},{0,48},{16,64},{32,80},{48,96},{64,112},... | collective-permute-start | bytes 497672 | tf_op jit(solution)/shard_map/ppermute | solution.py:13
  234.5 12.7 %collective-permute-start.1 = (f32[18,2304]{1,0:T(8,128)S(1)}, f32[18,2304]{1,0:T(8,128)S(1)}, u32[]{:S(2)}, u32[]{:S(2)}) collective-permute-start(f32[18,2304]{1,0:T(8,128)S(1)} %get-tuple-element.6), channel_id=1, source_target_pairs={{480,0},{496,16},{0,32},{16,48},{32,64},{48,80},{64,96},{80,112},{... | collective-permute-start | bytes 497672 | tf_op jit(solution)/shard_map/ppermute | solution.py:13
  237.9 14.0 %collective-permute-start = (f32[18,2304]{1,0:T(8,128)S(1)}, f32[18,2304]{1,0:T(8,128)S(1)}, u32[]{:S(2)}, u32[]{:S(2)}) collective-permute-start(f32[18,2304]{1,0:T(8,128)S(1)} %get-tuple-element.4), channel_id=1, source_target_pairs={{496,0},{0,16},{16,32},{32,48},{48,64},{64,80},{80,96},{96,112},{1... | collective-permute-start | bytes 497672 | tf_op jit(solution)/shard_map/ppermute | solution.py:13
Sparse Core Ops, SparseCore 0:
  119.9 108.9 all-reduce.2
where the time goes:
time: 261 us; the launch traced here: 260 us
  waiting for transfers between devices  120 us (46%)
  blocking collectives  51.2 us (20%)
  local copies, waits for them, and re-layouts  29.6 us (11%)
  starting transfers between devices  25.3 us (10%)
  matrix products  16.1 us (6%)
  between operations  14.3 us (5%)
  other arithmetic  3.9 us (1%)
    psum x1, waiting for transfers between devices, shards(): summed = lax.psum(extended, 'band')  109 us
    psum x1, blocking collectives, shards(): band_total = lax.psum(partial_sum, 'band')  51.2 us
    ppermute x6, starting transfers between devices, shifted(): return lax.ppermute(block, axis, route)  25.3 us
    unnamed x13, local copies, waits for them, and re-layouts  15.7 us
    ppermute x6, waiting for transfers between devices, shifted(): return lax.ppermute(block, axis, route)  10.9 us
    dot_general x1, local copies, waits for them, and re-layouts, shards(): lax.dot_general(stacked, flat_tables, (((0,), (0,)), ((), ())), preferred...  7.83 us
    dot_general x1, matrix products, shards(): lax.dot_general(stacked, flat_tables, (((0,), (0,)), ((), ())), preferred...  5.99 us
  transfers between devices with their start and end apart: 7, of which 3 were waited for; matrix products, arithmetic and copies ran while one was open for 11% of the time, Pallas kernels for 0%

commit v1 on v0

v1 whole, which is shorter than its diff:
```python
import jax
import jax.numpy as jnp
from jax import lax
from jax.experimental import pallas as pl
from jax.experimental.pallas import tpu as pltpu
from jax.sharding import PartitionSpec as P

GX = 48
GXY = 2304
NH = 18
NPAIR = 171
DEPTH = 3
CZ = 18
ATOMS = 16
BAND = 16
SLAB = 32
PAD_P = 176
ROWS = 2 * PAD_P
OWNERS = 6
WIDE = GXY // OWNERS
WINDOW = 24
F32 = jnp.float32
BF16 = jnp.bfloat16
NT = (((1,), (1,)), ((), ()))


def iota(shape, axis):
    return lax.broadcasted_iota(jnp.int32, shape, axis)


def dot(a, b):
    return jnp.dot(a, b, preferred_element_type=F32)


def dot_nt(a, b):
    return lax.dot_general(a, b, NT, preferred_element_type=F32)


def split(x, terms):
    parts = []
    for _ in range(terms):
        part = x.astype(BF16)
        parts.append(part)
        x = x - part.astype(F32)
    return parts


def column(row):
    picked = jnp.where(iota((ATOMS, ATOMS), 0) == iota((ATOMS, ATOMS), 1), row.astype(F32), 0.0)
    return jnp.sum(picked, axis=1, keepdims=True).astype(jnp.int32)


def rotate(values, amount, left):
    amount = jnp.broadcast_to(amount, values.shape)
    for bit in range(12):
        step = 1 << bit
        turned = pltpu.roll(values, GXY - step if left else step, 1)
        values = jnp.where((amount & step) != 0, turned, values)
    return values


def remote(src, dst, send, recv, **where):
    return pltpu.make_async_remote_copy(
        src_ref=src,
        dst_ref=dst,
        send_sem=send,
        recv_sem=recv,
        device_id=where,
        device_id_type=pl.DeviceIdType.MESH,
    )


def kernel(
    pt, occ, root, xy, kind, pot, tab, dens, ints,
    raw, tables, bt, rs1, tt, pex, pout, pin, boxes, ext, rs3, st, p4, exq, ag, isnd, ircv,
    tab_sem, s1, r1, s2, r2, sp, rp, s3, r3, s4, r4, s5, r5, s6, r6,
):
    me = lax.axis_index("band")
    slab = lax.axis_index("slab")

    def peer(rel):
        return lax.rem(me + rel, BAND)

    barrier = pltpu.get_barrier_semaphore()

    def greet(rel, carry):
        pl.semaphore_signal(
            barrier, inc=1, device_id={"band": peer(rel)}, device_id_type=pl.DeviceIdType.MESH
        )
        return carry

    lax.fori_loop(1, BAND, greet, 0)
    for k in (1, 2, 3, SLAB - 3, SLAB - 2, SLAB - 1):
        pl.semaphore_signal(
            barrier, inc=1, device_id={"slab": lax.rem(slab + k, SLAB)},
            device_id_type=pl.DeviceIdType.MESH,
        )
    fetch = pltpu.make_async_copy(tab, raw.at[pl.ds(0, NPAIR)], tab_sem)
    fetch.start()

    p = pt[...]
    weighted = split(p.astype(F32) * occ[...], 2)
    gram = dot_nt(weighted[0], p) + dot_nt(weighted[1], p)
    size = NH * ATOMS
    same = (iota((size, size), 0) & 15) == (iota((size, size), 1) & 15)
    pair = iota((1, 256), 1)
    i_of = jnp.zeros((1, 256), jnp.int32)
    start = jnp.zeros((1, 256), jnp.int32)
    for i in range(1, NH):
        past = pair >= i * NH - i * (i - 1) // 2
        i_of = i_of + jnp.where(past, 1, 0)
        start = start + jnp.where(past, NH - i + 1, 0)
    j_of = pair - start + i_of
    pick_j = jnp.where((iota((size, 256), 0) >> 4) == j_of, 1.0, 0.0).astype(BF16)
    spread = jnp.zeros((size, 256), F32)
    for part in split(jnp.where(same, gram, 0.0), 3):
        spread = spread + dot(part, pick_j)
    partial = jnp.zeros((ATOMS, 256), F32)
    for i in range(NH):
        partial = partial + jnp.where(i_of == i, spread[i * ATOMS : (i + 1) * ATOMS], 0.0)
    partial = partial * jnp.where(i_of == j_of, 1.0, 2.0)
    for t in range(4):
        bt[t] = partial[t // 2 * 8 : t // 2 * 8 + 8, t % 2 * 128 : t % 2 * 128 + 128]

    pl.semaphore_wait(barrier, BAND - 1 + 6)

    def send1(t):
        return remote(bt.at[t], rs1.at[me], s1.at[t], r1.at[me], band=4 * t)

    for t in range(4):
        @pl.when(me != 4 * t)
        def _(t=t):
            send1(t).start()

        @pl.when(me == 4 * t)
        def _(t=t):
            rs1[me] = bt[t]

    pout[:, 0:GXY] = pot[0:16, :].astype(BF16)
    pex[...] = jnp.zeros(pex.shape, F32)
    for r in range(2):
        for c in range(6):
            pex[r * 6 + c : r * 6 + c + 1, :] = pot[16 + r : 17 + r, c * 384 : c * 384 + 384]
    pout[:, GXY : GXY + 384] = pex[...].astype(BF16)
    near = me // 6
    first = DEPTH * me - CZ * near

    def send_pot(half):
        return remote(
            pout, pin.at[half], sp.at[half], rp.at[half],
            slab=lax.rem(slab + SLAB - near - half, SLAB),
        )

    @pl.when(near != 0)
    def _():
        send_pot(0).start()

    @pl.when(near == 0)
    def _():
        pin[0] = pout[...]

    send_pot(1).start()

    tile = me // 4

    def wait1(rel, carry):
        other = peer(rel)
        remote(bt.at[0], rs1.at[other], s1.at[0], r1.at[other], band=other).wait_recv()
        return carry

    def send2(rel):
        return remote(tt.at[tile], tt.at[tile], s2.at[rel], r2.at[tile], band=peer(rel))

    def start2(rel, carry):
        send2(rel).start()
        return carry

    @pl.when(lax.rem(me, 4) == 0)
    def _():
        lax.fori_loop(1, BAND, wait1, 0)
        tt[tile] = jnp.sum(rs1[...], axis=0)
        lax.fori_loop(1, BAND, start2, 0)

    raw[NPAIR:PAD_P] = jnp.zeros((PAD_P - NPAIR, DEPTH, 2, GXY), BF16)
    fetch.wait()

    def regroup(block, carry):
        for d in range(DEPTH):
            rows = raw[pl.ds(block * 8, 8), d]
            tables[d, pl.ds(pl.multiple_of(block * 16, 16), 16), :] = rows.reshape(16, GXY)
        return carry

    lax.fori_loop(0, PAD_P // 8, regroup, 0)

    offset_row = root[...] - slab * CZ
    offset = column(offset_row)
    anchor = column(xy[...])
    species = column(kind[...])
    corner = anchor - GX * ((anchor.astype(F32) + 0.5) * (1.0 / GX)).astype(jnp.int32)
    lane = iota((ATOMS, GXY), 1)
    line = lane - GX * ((lane.astype(F32) + 0.5) * (1.0 / GX)).astype(jnp.int32)
    corner = jnp.broadcast_to(corner, (ATOMS, GXY))
    mine = jnp.broadcast_to(species, (ATOMS, ROWS)) == (iota((ATOMS, ROWS), 1) & 1)
    to_rows = jnp.where((iota((256, ROWS), 1) >> 1) == iota((256, ROWS), 0), 1.0, 0.0).astype(BF16)

    @pl.when(near != 0)
    def _():
        send_pot(0).wait_recv()

    send_pot(1).wait_recv()
    extra = []
    for half in range(2):
        packed_rows = pin[half, :, GXY : GXY + 384].astype(F32)
        for r in range(2):
            extra.append(
                jnp.concatenate([packed_rows[r * 6 + c : r * 6 + c + 1] for c in range(6)], axis=1)
            )
    extra = jnp.concatenate(extra + [jnp.zeros((12, GXY), F32)], axis=0).astype(BF16)
    planes = jnp.concatenate([pin[0, :, 0:GXY], pin[1, :, 0:GXY], extra], axis=0)
    for d in range(DEPTH):
        target = offset + (first + d)
        late = jnp.where(target >= CZ, 1, 0)
        row = target - CZ * late
        source = jnp.where(row < 16, 16 * late + row, 32 + 2 * late + row - 16)
        choose = jnp.where(
            iota((ATOMS, 48), 1) == jnp.broadcast_to(source, (ATOMS, 48)), 1.0, 0.0
        ).astype(BF16)
        turned = rotate(dot(choose, planes), anchor, True)
        turned = jnp.where(line < GX - corner, turned, pltpu.roll(turned, GX, 1))
        boxes[d] = turned.astype(BF16)

    for t in range(4):
        @pl.when(me != 4 * t)
        def _(t=t):
            remote(tt.at[t], tt.at[t], s2.at[0], r2.at[t], band=4 * t).wait_recv()

    packed = jnp.concatenate(
        [
            jnp.concatenate([tt[0], tt[1]], axis=1),
            jnp.concatenate([tt[2], tt[3]], axis=1),
        ],
        axis=0,
    ).astype(BF16)
    left = jnp.where(mine, dot(packed, to_rows), 0.0).astype(BF16)
    window = jnp.zeros((WINDOW, GXY), F32)
    for d in range(DEPTH):
        placed = rotate(dot(left, tables[d]), anchor, False)
        placed = jnp.where(line >= corner, placed, pltpu.roll(placed, GXY - GX, 1))
        onto = jnp.where(iota((WINDOW, ATOMS), 0) == offset_row + d, 1.0, 0.0).astype(BF16)
        for part in split(placed, 2):
            window = window + dot(onto, part)
    for j in range(OWNERS):
        ext[j] = window[:, j * WIDE : (j + 1) * WIDE]

    def send3(j):
        return remote(ext.at[j], rs3.at[me], s3.at[j], r3.at[me], band=8 * j // 3)

    for j in range(OWNERS):
        @pl.when(me != 8 * j // 3)
        def _(j=j):
            send3(j).start()

        @pl.when(me == 8 * j // 3)
        def _(j=j):
            rs3[me] = ext[j]

    sums = jnp.zeros((ATOMS, ROWS), F32)
    for d in range(DEPTH):
        sums = sums + dot_nt(boxes[d], tables[d])
    folded = jnp.zeros((ATOMS, 256), F32)
    for part in split(jnp.where(mine, sums, 0.0), 3):
        folded = folded + dot_nt(part, to_rows)
    for a in range(ATOMS):
        isnd[a] = folded[a : a + 1]

    def send6(rel):
        other = peer(rel)
        return remote(isnd.at[other], ircv.at[me], s6.at[rel], r6.at[me], band=other)

    def start6(rel, carry):
        send6(rel).start()
        return carry

    lax.fori_loop(1, BAND, start6, 0)
    ircv[me] = isnd[me]

    mark = (3 * me + 7) // 8
    owner = jnp.logical_and(mark < OWNERS, 8 * mark // 3 == me)
    own = jnp.minimum(mark, OWNERS - 1)

    def wait3(rel, carry):
        other = peer(rel)
        remote(ext.at[0], rs3.at[other], s3.at[0], r3.at[other], band=other).wait_recv()
        return carry

    def send4(k):
        return remote(
            st.at[k], p4.at[k - 1], s4.at[k - 1], r4.at[k - 1], slab=lax.rem(slab + k, SLAB)
        )

    def send5(rel):
        return remote(ag.at[own], ag.at[own], s5.at[rel], r5.at[own], band=peer(rel))

    def start5(rel, carry):
        send5(rel).start()
        return carry

    @pl.when(owner)
    def _():
        st[...] = jnp.zeros(st.shape, F32)
        lax.fori_loop(1, BAND, wait3, 0)
        for member in range(BAND):
            k, row = divmod(member * DEPTH, CZ)
            head = min(CZ - row, 20)
            st[k, row : row + head, :] += rs3[member, 0:head, :]
            if head < 20:
                st[k + 1, 0 : 20 - head, :] += rs3[member, head:20, :]
        for k in (1, 2, 3):
            send4(k).start()
        for k in (1, 2, 3):
            send4(k).wait_recv()
        total = st[0] + p4[0] + p4[1] + p4[2]
        exq[...] = jnp.zeros(exq.shape, F32)
        for r in range(2):
            for c in range(3):
                exq[r * 3 + c : r * 3 + c + 1, :] = total[16 + r : 17 + r, c * 128 : c * 128 + 128]
        ag[own, :, 0:WIDE] = total[0:16].astype(BF16)
        ag[own, :, WIDE : WIDE + 128] = exq[...].astype(BF16)
        lax.fori_loop(1, BAND, start5, 0)

    def wait6(rel, carry):
        other = peer(rel)
        remote(isnd.at[0], ircv.at[other], s6.at[0], r6.at[other], band=other).wait_recv()
        return carry

    lax.fori_loop(1, BAND, wait6, 0)
    ints[...] = jnp.sum(ircv[...], axis=0)[:, 0:NPAIR]

    for j in range(OWNERS):
        @pl.when(me != 8 * j // 3)
        def _(j=j):
            remote(ag.at[j], ag.at[j], s5.at[0], r5.at[j], band=8 * j // 3).wait_recv()

        dens[0:16, j * WIDE : (j + 1) * WIDE] = ag[j, :, 0:WIDE].astype(F32)
        tail = ag[j, :, WIDE : WIDE + 128].astype(F32)
        for r in range(2):
            for c in range(3):
                at = j * WIDE + c * 128
                dens[16 + r : 17 + r, at : at + 128] = tail[r * 3 + c : r * 3 + c + 1]

    for t in range(4):
        @pl.when(me != 4 * t)
        def _(t=t):
            send1(t).wait_send()

    @pl.when(near != 0)
    def _():
        send_pot(0).wait_send()

    send_pot(1).wait_send()

    def end2(rel, carry):
        send2(rel).wait_send()
        return carry

    @pl.when(lax.rem(me, 4) == 0)
    def _():
        lax.fori_loop(1, BAND, end2, 0)

    for j in range(OWNERS):
        @pl.when(me != 8 * j // 3)
        def _(j=j):
            send3(j).wait_send()

    def end6(rel, carry):
        send6(rel).wait_send()
        return carry

    lax.fori_loop(1, BAND, end6, 0)

    def end5(rel, carry):
        send5(rel).wait_send()
        return carry

    @pl.when(owner)
    def _():
        for k in (1, 2, 3):
            send4(k).wait_send()
        lax.fori_loop(1, BAND, end5, 0)


def shards(projections, occupation, augment_tables, box_root, box_xy, species, potential):
    pt = jnp.transpose(projections, (1, 2, 0)).reshape(NH * ATOMS, 256)
    tab = jnp.transpose(augment_tables, (1, 2, 0, 3))
    vmem = pl.BlockSpec(memory_space=pltpu.VMEM)
    dma = pltpu.SemaphoreType.DMA
    density, integrals = pl.pallas_call(
        kernel,
        out_shape=(
            jax.ShapeDtypeStruct((CZ, GXY), F32),
            jax.ShapeDtypeStruct((1, NPAIR), F32),
        ),
        in_specs=[vmem] * 6 + [pl.BlockSpec(memory_space=pl.ANY)],
        out_specs=(vmem, vmem),
        scratch_shapes=[
            pltpu.VMEM((PAD_P, DEPTH, 2, GXY), BF16),
            pltpu.VMEM((DEPTH, ROWS, GXY), BF16),
            pltpu.VMEM((4, 8, 128), F32),
            pltpu.VMEM((BAND, 8, 128), F32),
            pltpu.VMEM((4, 8, 128), F32),
            pltpu.VMEM((16, 384), F32),
            pltpu.VMEM((16, GXY + 384), BF16),
            pltpu.VMEM((2, 16, GXY + 384), BF16),
            pltpu.VMEM((DEPTH, ATOMS, GXY), BF16),
            pltpu.VMEM((OWNERS, WINDOW, WIDE), F32),
            pltpu.VMEM((BAND, WINDOW, WIDE), F32),
            pltpu.VMEM((4, WINDOW, WIDE), F32),
            pltpu.VMEM((3, WINDOW, WIDE), F32),
            pltpu.VMEM((16, 128), F32),
            pltpu.VMEM((OWNERS, 16, WIDE + 128), BF16),
            pltpu.VMEM((ATOMS, 1, 256), F32),
            pltpu.VMEM((BAND, 1, 256), F32),
            dma,
            dma((4,)), dma((BAND,)),
            dma((BAND,)), dma((4,)),
            dma((2,)), dma((2,)),
            dma((OWNERS,)), dma((BAND,)),
            dma((3,)), dma((3,)),
            dma((BAND,)), dma((OWNERS,)),
            dma((BAND,)), dma((BAND,)),
        ],
        compiler_params=pltpu.CompilerParams(
            collective_id=0, has_side_effects=True, vmem_limit_bytes=40 << 20
        ),
    )(
        pt,
        occupation.reshape(1, 256),
        box_root.reshape(1, ATOMS),
        box_xy.reshape(1, ATOMS),
        species.reshape(1, ATOMS),
        potential,
        tab,
    )
    return density, integrals.reshape(NPAIR, 1)


def solution(mesh):
    placed = (
        P("band", None, "slab"),
        P("band"),
        P(None, None, "band", None),
        P("slab"),
        P("slab"),
        P("slab"),
        P("slab", None),
    )
    return jax.shard_map(
        shards,
        mesh=mesh,
        in_specs=placed,
        out_specs=(P("slab", None), P(None, ("slab", "band"))),
        check_vma=False,
    )
```

time: 261 us -> 56.9 us (0.22)
  waiting for transfers between devices: 120 us -> 0 us
  blocking collectives: 51.2 us -> 0 us
  Pallas kernels: 0 us -> 47.9 us
  starting transfers between devices: 25.3 us -> 0 us
  local copies, waits for them, and re-layouts: 29.6 us -> 8.07 us
  matrix products: 16.1 us -> 0 us
  between operations: 14.3 us -> 0.66 us
  other arithmetic: 3.9 us -> 0 us
    psum x1 -> x0, waiting for transfers between devices: 109 us -> none  [shards(): summed = lax.psum(extended, 'band')]
    psum x1 -> x0, blocking collectives: 51.2 us -> none  [shards(): band_total = lax.psum(partial_sum, 'band')]
    pallas_call x0 -> x1, Pallas kernels: none -> 47.9 us  [shards(): pl.pallas_call(kernel, out_shape=(jax.ShapeDtypeStruct((CZ, GXY), F32), j...]
    ppermute x6 -> x0, starting transfers between devices: 25.3 us -> none  [shifted(): return lax.ppermute(block, axis, route)]
    dot_general x8 -> x0, matrix products: 16.1 us -> none  [the longest x1 5.99 us: shards(): lax.dot_general(stacked, flat_tables, (((0,), (0,)), ((), ())), preferred...]
    ppermute x6 -> x0, waiting for transfers between devices: 10.9 us -> none  [shifted(): return lax.ppermute(block, axis, route)]
    dot_general x1 -> x0, local copies, waits for them, and re-layouts: 7.83 us -> none  [shards(): lax.dot_general(stacked, flat_tables, (((0,), (0,)), ((), ())), preferred...]
    unnamed x13 -> x16, local copies, waits for them, and re-layouts: 15.7 us -> 8.07 us
  transfers between devices with their start and end apart: 7 -> 0, of which waited for: 3 -> 0; matrix products, arithmetic and copies ran while one was open for 11% -> 0% of each run, Pallas kernels for 0% -> 0%
where the time goes in v1:
time: 56.9 us; the launch traced here: 56.6 us
  Pallas kernels  47.9 us (84%)
  local copies, waits for them, and re-layouts  8.07 us (14%)
  between operations  0.66 us (1%)
    pallas_call x1, Pallas kernels, shards(): pl.pallas_call(kernel, out_shape=(jax.ShapeDtypeStruct((CZ, GXY), F32), j...  47.9 us
    unnamed x16, local copies, waits for them, and re-layouts  8.07 us

profile of v1, /device:TPU:1, one launch (start us, length us, event | category | flops | bytes accessed | tf_op | source)
XLA Modules:
  0.0 56.6 jit_solution(10754312310645806863)
XLA Ops:
  0.6 0.0 copy-start
  0.6 2.3 %copy-done = bf16[2,171,3,2304]{3,0,2,1:T(2,128)(2,1)S(1)} copy-done((bf16[2,171,3,2304]{3,0,2,1:T(2,128)(2,1)S(1)}, bf16[2,171,3,2304]{3,0,2,1:T(2,128)(2,1)}, u32[]{:S(2)}) %copy-start) | copy-done | bytes 4727832
  3.0 0.0 copy-start.1
  3.0 0.9 %copy-done.1 = f32[18,2304]{1,0:T(8,128)S(1)} copy-done((f32[18,2304]{1,0:T(8,128)S(1)}, f32[18,2304]{1,0:T(8,128)}, u32[]{:S(2)}) %copy-start.1) | copy-done | bytes 165912
  3.9 0.0 copy-start.2
  3.9 0.9 %copy-done.2 = bf16[256,18,16]{0,2,1:T(8,128)(2,1)S(1)} copy-done((bf16[256,18,16]{0,2,1:T(8,128)(2,1)S(1)}, bf16[256,18,16]{0,2,1:T(8,128)(2,1)}, u32[]{:S(2)}) %copy-start.2) | copy-done | bytes 147480
  4.8 0.0 copy-start.3
  4.8 0.7 %copy-done.3 = f32[256]{0:T(256)S(1)} copy-done((f32[256]{0:T(256)S(1)}, f32[256]{0:T(256)}, u32[]{:S(2)}) %copy-start.3) | copy-done | bytes 1048
  5.5 0.0 copy-start.4
  5.5 0.7 %copy-done.4 = s32[16]{0:T(128)S(1)} copy-done((s32[16]{0:T(128)S(1)}, s32[16]{0:T(128)}, u32[]{:S(2)}) %copy-start.4) | copy-done | bytes 88
  6.2 0.0 copy-start.5
  6.2 0.7 %copy-done.5 = s32[16]{0:T(128)S(1)} copy-done((s32[16]{0:T(128)S(1)}, s32[16]{0:T(128)}, u32[]{:S(2)}) %copy-start.5) | copy-done | bytes 88
  6.8 0.0 copy-start.6
  6.8 0.7 %copy-done.6 = s32[16]{0:T(128)S(1)} copy-done((s32[16]{0:T(128)S(1)}, s32[16]{0:T(128)}, u32[]{:S(2)}) %copy-start.6) | copy-done | bytes 88
  7.5 47.9 %shard_map.86 = (f32[18,2304]{1,0:T(8,128)S(1)}, f32[1,171]{1,0:T(1,128)S(1)}) custom-call(bf16[288,256]{1,0:T(8,128)(2,1)S(1)} %bitcast.10, f32[1,256]{1,0:T(1,128)S(1)} %bitcast.12, s32[1,16]{1,0:T(1,128)S(1)} %bitcast.13, s32[1,16]{1,0:T(1,128)S(1)} %bitcast.14, s32[1,16]{1,0:T(1,128)S(1)} %bitcast.15, f32[18,2304]{1,0:T(8,128)S(1)} %copy-done.1, ...), custom_call_target="tpu_custom_call" | custom-call | tf_op jit(solution)/shard_map/pallas_call | solution.py:397
  55.4 0.7 %copy.11 = f32[18,2304]{1,0:T(8,128)} copy(f32[18,2304]{1,0:T(8,128)S(1)} %get-tuple-element.8) | data formatting | bytes 331776
  56.0 0.6 copy.12
Async XLA Ops:
  0.6 2.3 %copy-start = (bf16[2,171,3,2304]{3,0,2,1:T(2,128)(2,1)S(1)}, bf16[2,171,3,2304]{3,0,2,1:T(2,128)(2,1)}, u32[]{:S(2)}) copy-start(bf16[2,171,3,2304]{3,0,2,1:T(2,128)(2,1)} %param.9) | copy-start | bytes 14183428
  3.0 0.9 %copy-start.1 = (f32[18,2304]{1,0:T(8,128)S(1)}, f32[18,2304]{1,0:T(8,128)}, u32[]{:S(2)}) copy-start(f32[18,2304]{1,0:T(8,128)} %pot.1) | copy-start | bytes 497668
  3.9 0.9 %copy-start.2 = (bf16[256,18,16]{0,2,1:T(8,128)(2,1)S(1)}, bf16[256,18,16]{0,2,1:T(8,128)(2,1)}, u32[]{:S(2)}) copy-start(bf16[256,18,16]{0,2,1:T(8,128)(2,1)} %param.7) | copy-start | bytes 442372
  4.8 0.7 %copy-start.3 = (f32[256]{0:T(256)S(1)}, f32[256]{0:T(256)}, u32[]{:S(2)}) copy-start(f32[256]{0:T(256)} %param.8) | copy-start | bytes 3076
  5.5 0.7 %copy-start.4 = (s32[16]{0:T(128)S(1)}, s32[16]{0:T(128)}, u32[]{:S(2)}) copy-start(s32[16]{0:T(128)} %param.10) | copy-start | bytes 196
  6.2 0.7 %copy-start.5 = (s32[16]{0:T(128)S(1)}, s32[16]{0:T(128)}, u32[]{:S(2)}) copy-start(s32[16]{0:T(128)} %param.11) | copy-start | bytes 196
  6.8 0.7 %copy-start.6 = (s32[16]{0:T(128)S(1)}, s32[16]{0:T(128)}, u32[]{:S(2)}) copy-start(s32[16]{0:T(128)} %param.12) | copy-start | bytes 196

commit v2 on v1

--- a/solution.py
+++ b/solution.py
@@ -19,6 +19,7 @@
 OWNERS = 6
 WIDE = GXY // OWNERS
 WINDOW = 24
+EARLY = 6
 F32 = jnp.float32
 BF16 = jnp.bfloat16
 NT = (((1,), (1,)), ((), ()))
@@ -71,9 +72,9 @@
 
 
 def kernel(
-    pt, occ, root, xy, kind, pot, tab, dens, ints,
-    raw, tables, bt, rs1, tt, pex, pout, pin, boxes, ext, rs3, st, p4, exq, ag, isnd, ircv,
-    tab_sem, s1, r1, s2, r2, sp, rp, s3, r3, s4, r4, s5, r5, s6, r6,
+    pt_hbm, occ_hbm, root_hbm, xy_hbm, kind_hbm, pot_hbm, tab, dens, ints,
+    pt, occ, root, xy, kind, pot, raw, tables, bt, rs1, tt, pex, pout, pin, boxes, ext, rs3, st, p4, exq, ag, isnd, ircv,
+    in_sem, tab_sem, s1, r1, s2, r2, sp, rp, s3, r3, s4, r4, s5, r5, s6, r6,
 ):
     me = lax.axis_index("band")
     slab = lax.axis_index("slab")
@@ -95,12 +96,17 @@
             barrier, inc=1, device_id={"slab": lax.rem(slab + k, SLAB)},
             device_id_type=pl.DeviceIdType.MESH,
         )
+    loads = [
+        pltpu.make_async_copy(src, dst, in_sem.at[n])
+        for n, (src, dst) in enumerate(
+            [(pt_hbm, pt), (occ_hbm, occ), (pot_hbm, pot), (root_hbm, root), (xy_hbm, xy), (kind_hbm, kind)]
+        )
+    ]
+    for load in loads:
+        load.start()
     fetch = pltpu.make_async_copy(tab, raw.at[pl.ds(0, NPAIR)], tab_sem)
     fetch.start()
 
-    p = pt[...]
-    weighted = split(p.astype(F32) * occ[...], 2)
-    gram = dot_nt(weighted[0], p) + dot_nt(weighted[1], p)
     size = NH * ATOMS
     same = (iota((size, size), 0) & 15) == (iota((size, size), 1) & 15)
     pair = iota((1, 256), 1)
@@ -112,6 +118,11 @@
         start = start + jnp.where(past, NH - i + 1, 0)
     j_of = pair - start + i_of
     pick_j = jnp.where((iota((size, 256), 0) >> 4) == j_of, 1.0, 0.0).astype(BF16)
+    loads[0].wait()
+    loads[1].wait()
+    p = pt[...]
+    weighted = split(p.astype(F32) * occ[...], 2)
+    gram = dot_nt(weighted[0], p) + dot_nt(weighted[1], p)
     spread = jnp.zeros((size, 256), F32)
     for part in split(jnp.where(same, gram, 0.0), 3):
         spread = spread + dot(part, pick_j)
@@ -136,6 +147,7 @@
         def _(t=t):
             rs1[me] = bt[t]
 
+    loads[2].wait()
     pout[:, 0:GXY] = pot[0:16, :].astype(BF16)
     pex[...] = jnp.zeros(pex.shape, F32)
     for r in range(2):
@@ -161,26 +173,6 @@
 
     send_pot(1).start()
 
-    tile = me // 4
-
-    def wait1(rel, carry):
-        other = peer(rel)
-        remote(bt.at[0], rs1.at[other], s1.at[0], r1.at[other], band=other).wait_recv()
-        return carry
-
-    def send2(rel):
-        return remote(tt.at[tile], tt.at[tile], s2.at[rel], r2.at[tile], band=peer(rel))
-
-    def start2(rel, carry):
-        send2(rel).start()
-        return carry
-
-    @pl.when(lax.rem(me, 4) == 0)
-    def _():
-        lax.fori_loop(1, BAND, wait1, 0)
-        tt[tile] = jnp.sum(rs1[...], axis=0)
-        lax.fori_loop(1, BAND, start2, 0)
-
     raw[NPAIR:PAD_P] = jnp.zeros((PAD_P - NPAIR, DEPTH, 2, GXY), BF16)
     fetch.wait()
 
@@ -190,7 +182,31 @@
             tables[d, pl.ds(pl.multiple_of(block * 16, 16), 16), :] = rows.reshape(16, GXY)
         return carry
 
-    lax.fori_loop(0, PAD_P // 8, regroup, 0)
+    lax.fori_loop(0, EARLY, regroup, 0)
+
+    tile = me // 4
+
+    def wait1(rel, carry):
+        other = peer(rel)
+        remote(bt.at[0], rs1.at[other], s1.at[0], r1.at[other], band=other).wait_recv()
+        return carry
+
+    def send2(rel):
+        return remote(tt.at[tile], tt.at[tile], s2.at[rel], r2.at[tile], band=peer(rel))
+
+    def start2(rel, carry):
+        send2(rel).start()
+        return carry
+
+    @pl.when(lax.rem(me, 4) == 0)
+    def _():
+        lax.fori_loop(1, BAND, wait1, 0)
+        tt[tile] = jnp.sum(rs1[...], axis=0)
+        lax.fori_loop(1, BAND, start2, 0)
+
+    lax.fori_loop(EARLY, PAD_P // 8, regroup, 0)
+    for load in loads[3:]:
+        load.wait()
 
     offset_row = root[...] - slab * CZ
     offset = column(offset_row)
@@ -202,6 +218,41 @@
     corner = jnp.broadcast_to(corner, (ATOMS, GXY))
     mine = jnp.broadcast_to(species, (ATOMS, ROWS)) == (iota((ATOMS, ROWS), 1) & 1)
     to_rows = jnp.where((iota((256, ROWS), 1) >> 1) == iota((256, ROWS), 0), 1.0, 0.0).astype(BF16)
+
+    for t in range(4):
+        @pl.when(me != 4 * t)
+        def _(t=t):
+            remote(tt.at[t], tt.at[t], s2.at[0], r2.at[t], band=4 * t).wait_recv()
+
+    packed = jnp.concatenate(
+        [
+            jnp.concatenate([tt[0], tt[1]], axis=1),
+            jnp.concatenate([tt[2], tt[3]], axis=1),
+        ],
+        axis=0,
+    ).astype(BF16)
+    left = jnp.where(mine, dot(packed, to_rows), 0.0).astype(BF16)
+    window = jnp.zeros((WINDOW, GXY), F32)
+    for d in range(DEPTH):
+        placed = rotate(dot(left, tables[d]), anchor, False)
+        placed = jnp.where(line >= corner, placed, pltpu.roll(placed, GXY - GX, 1))
+        onto = jnp.where(iota((WINDOW, ATOMS), 0) == offset_row + d, 1.0, 0.0).astype(BF16)
+        for part in split(placed, 2):
+            window = window + dot(onto, part)
+    for j in range(OWNERS):
+        ext[j] = window[:, j * WIDE : (j + 1) * WIDE]
+
+    def send3(j):
+        return remote(ext.at[j], rs3.at[me], s3.at[j], r3.at[me], band=8 * j // 3)
+
+    for j in range(OWNERS):
+        @pl.when(me != 8 * j // 3)
+        def _(j=j):
+            send3(j).start()
+
+        @pl.when(me == 8 * j // 3)
+        def _(j=j):
+            rs3[me] = ext[j]
 
     @pl.when(near != 0)
     def _():
@@ -229,41 +280,6 @@
         turned = jnp.where(line < GX - corner, turned, pltpu.roll(turned, GX, 1))
         boxes[d] = turned.astype(BF16)
 
-    for t in range(4):
-        @pl.when(me != 4 * t)
-        def _(t=t):
-            remote(tt.at[t], tt.at[t], s2.at[0], r2.at[t], band=4 * t).wait_recv()
-
-    packed = jnp.concatenate(
-        [
-            jnp.concatenate([tt[0], tt[1]], axis=1),
-            jnp.concatenate([tt[2], tt[3]], axis=1),
-        ],
-        axis=0,
-    ).astype(BF16)
-    left = jnp.where(mine, dot(packed, to_rows), 0.0).astype(BF16)
-    window = jnp.zeros((WINDOW, GXY), F32)
-    for d in range(DEPTH):
-        placed = rotate(dot(left, tables[d]), anchor, False)
-        placed = jnp.where(line >= corner, placed, pltpu.roll(placed, GXY - GX, 1))
-        onto = jnp.where(iota((WINDOW, ATOMS), 0) == offset_row + d, 1.0, 0.0).astype(BF16)
-        for part in split(placed, 2):
-            window = window + dot(onto, part)
-    for j in range(OWNERS):
-        ext[j] = window[:, j * WIDE : (j + 1) * WIDE]
-
-    def send3(j):
-        return remote(ext.at[j], rs3.at[me], s3.at[j], r3.at[me], band=8 * j // 3)
-
-    for j in range(OWNERS):
-        @pl.when(me != 8 * j // 3)
-        def _(j=j):
-            send3(j).start()
-
-        @pl.when(me == 8 * j // 3)
-        def _(j=j):
-            rs3[me] = ext[j]
-
     sums = jnp.zeros((ATOMS, ROWS), F32)
     for d in range(DEPTH):
         sums = sums + dot_nt(boxes[d], tables[d])
@@ -400,9 +416,15 @@
             jax.ShapeDtypeStruct((CZ, GXY), F32),
             jax.ShapeDtypeStruct((1, NPAIR), F32),
         ),
-        in_specs=[vmem] * 6 + [pl.BlockSpec(memory_space=pl.ANY)],
+        in_specs=[pl.BlockSpec(memory_space=pltpu.HBM)] * 7,
         out_specs=(vmem, vmem),
         scratch_shapes=[
+            pltpu.VMEM((NH * ATOMS, 256), BF16),
+            pltpu.VMEM((1, 256), F32),
+            pltpu.VMEM((1, ATOMS), jnp.int32),
+            pltpu.VMEM((1, ATOMS), jnp.int32),
+            pltpu.VMEM((1, ATOMS), jnp.int32),
+            pltpu.VMEM((CZ, GXY), F32),
             pltpu.VMEM((PAD_P, DEPTH, 2, GXY), BF16),
             pltpu.VMEM((DEPTH, ROWS, GXY), BF16),
             pltpu.VMEM((4, 8, 128), F32),
@@ -420,6 +442,7 @@
             pltpu.VMEM((OWNERS, 16, WIDE + 128), BF16),
             pltpu.VMEM((ATOMS, 1, 256), F32),
             pltpu.VMEM((BAND, 1, 256), F32),
+            dma((6,)),
             dma,
             dma((4,)), dma((BAND,)),
             dma((BAND,)), dma((4,)),
@@ -430,7 +453,7 @@
             dma((BAND,)), dma((BAND,)),
         ],
         compiler_params=pltpu.CompilerParams(
-            collective_id=0, has_side_effects=True, vmem_limit_bytes=40 << 20
+            collective_id=0, has_side_effects=True, vmem_limit_bytes=56 << 20
         ),
     )(
         pt,

time: 56.9 us -> 52.4 us (0.921)
  local copies, waits for them, and re-layouts: 8.07 us -> 2.83 us
  Pallas kernels: 47.9 us -> 48.8 us
    unnamed x16 -> x2, local copies, waits for them, and re-layouts: 8.07 us -> 2.83 us
    pallas_call x1, Pallas kernels: 47.9 us -> 48.8 us  [shards(): pl.pallas_call(kernel, out_shape=(jax.ShapeDtypeStruct((CZ, GXY), F32), j...]
where the time goes in v2:
time: 52.4 us; the launch traced here: 52.2 us
  Pallas kernels  48.8 us (93%)
  local copies, waits for them, and re-layouts  2.83 us (5%)
  between operations  0.64 us (1%)
    pallas_call x1, Pallas kernels, shards(): pl.pallas_call(kernel, out_shape=(jax.ShapeDtypeStruct((CZ, GXY), F32), j...  48.8 us
    unnamed x2, local copies, waits for them, and re-layouts  2.83 us

profile of v2, /device:TPU:1, one launch (start us, length us, event | category | flops | bytes accessed | tf_op | source)
XLA Modules:
  0.0 52.2 jit_solution(17762507017143487456)
XLA Ops:
  0.6 48.8 %shard_map.86 = (f32[18,2304]{1,0:T(8,128)}, f32[1,171]{1,0:T(1,128)}) custom-call(bf16[288,256]{1,0:T(8,128)(2,1)} %bitcast.10, f32[1,256]{1,0:T(1,128)} %bitcast.12, s32[1,16]{1,0:T(1,128)} %bitcast.13, s32[1,16]{1,0:T(1,128)} %bitcast.14, s32[1,16]{1,0:T(1,128)} %bitcast.15, f32[18,2304]{1,0:T(8,128)} %pot_hbm.1, bf16[171,3,2,2304]{3,2,1,0:T(2,128)(2,1)} %bitcast.9), custom_call_target="tpu_custom_call" | custom-call | tf_op jit(solution)/shard_map/pallas_call | solution.py:413
  49.4 1.6 %copy.11 = f32[18,2304]{1,0:T(8,128)} copy(f32[18,2304]{1,0:T(8,128)} %get-tuple-element.8) | data formatting | bytes 331776
  51.0 1.2 %copy.12 = f32[171,1]{0,1:T(1,128)} copy(f32[171,1]{0,1:T(1,128)} %bitcast.11) | data formatting | bytes 1368

commit v3 on v2

--- a/solution.py
+++ b/solution.py
@@ -19,7 +19,7 @@
 OWNERS = 6
 WIDE = GXY // OWNERS
 WINDOW = 24
-EARLY = 6
+TILES = 18
 F32 = jnp.float32
 BF16 = jnp.bfloat16
 NT = (((1,), (1,)), ((), ()))
@@ -49,6 +49,16 @@
 def column(row):
     picked = jnp.where(iota((ATOMS, ATOMS), 0) == iota((ATOMS, ATOMS), 1), row.astype(F32), 0.0)
     return jnp.sum(picked, axis=1, keepdims=True).astype(jnp.int32)
+
+
+def rows_of(tables, d, c):
+    return jnp.concatenate(
+        [tables[d, 2 * c].reshape(ROWS, 128), tables[d, 2 * c + 1].reshape(ROWS, 128)], axis=1
+    )
+
+
+def take(sem, landed):
+    pltpu.make_async_copy(landed, landed, sem).wait()
 
 
 def rotate(values, amount, left):
@@ -73,7 +83,7 @@
 
 def kernel(
     pt_hbm, occ_hbm, root_hbm, xy_hbm, kind_hbm, pot_hbm, tab, dens, ints,
-    pt, occ, root, xy, kind, pot, raw, tables, bt, rs1, tt, pex, pout, pin, boxes, ext, rs3, st, p4, exq, ag, isnd, ircv,
+    pt, occ, root, xy, kind, pot, tables, bt, rs1, tt, pex, pout, pin, boxes, ext, rs3, st, p4, exq, ag, isnd, ircv,
     in_sem, tab_sem, s1, r1, s2, r2, sp, rp, s3, r3, s4, r4, s5, r5, s6, r6,
 ):
     me = lax.axis_index("band")
@@ -104,8 +114,12 @@
     ]
     for load in loads:
         load.start()
-    fetch = pltpu.make_async_copy(tab, raw.at[pl.ds(0, NPAIR)], tab_sem)
-    fetch.start()
+    tables[:, :, NPAIR:PAD_P] = jnp.zeros((DEPTH, TILES, PAD_P - NPAIR, 2, 128), BF16)
+    for d in range(DEPTH):
+        for c in range(TILES):
+            pltpu.make_async_copy(
+                tab.at[:, d, c], tables.at[d, c, pl.ds(0, NPAIR)], tab_sem.at[d]
+            ).start()
 
     size = NH * ATOMS
     same = (iota((size, size), 0) & 15) == (iota((size, size), 1) & 15)
@@ -136,7 +150,7 @@
     pl.semaphore_wait(barrier, BAND - 1 + 6)
 
     def send1(t):
-        return remote(bt.at[t], rs1.at[me], s1.at[t], r1.at[me], band=4 * t)
+        return remote(bt.at[t], rs1.at[me], s1.at[t], r1.at[0], band=4 * t)
 
     for t in range(4):
         @pl.when(me != 4 * t)
@@ -173,26 +187,10 @@
 
     send_pot(1).start()
 
-    raw[NPAIR:PAD_P] = jnp.zeros((PAD_P - NPAIR, DEPTH, 2, GXY), BF16)
-    fetch.wait()
-
-    def regroup(block, carry):
-        for d in range(DEPTH):
-            rows = raw[pl.ds(block * 8, 8), d]
-            tables[d, pl.ds(pl.multiple_of(block * 16, 16), 16), :] = rows.reshape(16, GXY)
-        return carry
-
-    lax.fori_loop(0, EARLY, regroup, 0)
-
     tile = me // 4
 
-    def wait1(rel, carry):
-        other = peer(rel)
-        remote(bt.at[0], rs1.at[other], s1.at[0], r1.at[other], band=other).wait_recv()
-        return carry
-
     def send2(rel):
-        return remote(tt.at[tile], tt.at[tile], s2.at[rel], r2.at[tile], band=peer(rel))
+        return remote(tt.at[tile], tt.at[tile], s2.at[0], r2.at[tile], band=peer(rel))
 
     def start2(rel, carry):
         send2(rel).start()
@@ -200,11 +198,13 @@
 
     @pl.when(lax.rem(me, 4) == 0)
     def _():
-        lax.fori_loop(1, BAND, wait1, 0)
+        take(r1.at[0], rs1.at[pl.ds(0, BAND - 1)])
         tt[tile] = jnp.sum(rs1[...], axis=0)
         lax.fori_loop(1, BAND, start2, 0)
 
-    lax.fori_loop(EARLY, PAD_P // 8, regroup, 0)
+    for d in range(DEPTH):
+        part = tables.at[d, :, pl.ds(0, NPAIR)]
+        pltpu.make_async_copy(part, part, tab_sem.at[d]).wait()
     for load in loads[3:]:
         load.wait()
 
@@ -234,16 +234,20 @@
     left = jnp.where(mine, dot(packed, to_rows), 0.0).astype(BF16)
     window = jnp.zeros((WINDOW, GXY), F32)
     for d in range(DEPTH):
-        placed = rotate(dot(left, tables[d]), anchor, False)
+        terms = [dot(left, rows_of(tables, d, c)) for c in range(TILES // 2)]
+        placed = rotate(jnp.concatenate(terms, axis=1), anchor, False)
         placed = jnp.where(line >= corner, placed, pltpu.roll(placed, GXY - GX, 1))
         onto = jnp.where(iota((WINDOW, ATOMS), 0) == offset_row + d, 1.0, 0.0).astype(BF16)
         for part in split(placed, 2):
             window = window + dot(onto, part)
     for j in range(OWNERS):
-        ext[j] = window[:, j * WIDE : (j + 1) * WIDE]
+        ext[j, :, 0:WIDE] = window[0:16, j * WIDE : (j + 1) * WIDE].astype(BF16)
+        ends = [window[16:24, j * WIDE + c * 128 : j * WIDE + c * 128 + 128] for c in range(3)]
+        ends = jnp.concatenate([ends[0] + pltpu.roll(ends[1], 4, 0), ends[2]], axis=0)
+        ext[j, :, WIDE : WIDE + 128] = ends.astype(BF16)
 
     def send3(j):
-        return remote(ext.at[j], rs3.at[me], s3.at[j], r3.at[me], band=8 * j // 3)
+        return remote(ext.at[j], rs3.at[me], s3.at[j], r3.at[0], band=8 * j // 3)
 
     for j in range(OWNERS):
         @pl.when(me != 8 * j // 3)
@@ -280,9 +284,53 @@
         turned = jnp.where(line < GX - corner, turned, pltpu.roll(turned, GX, 1))
         boxes[d] = turned.astype(BF16)
 
+    mark = (3 * me + 7) // 8
+    owner = jnp.logical_and(mark < OWNERS, 8 * mark // 3 == me)
+    own = jnp.minimum(mark, OWNERS - 1)
+
+    def send4(k):
+        return remote(
+            st.at[k], p4.at[k - 1], s4.at[k - 1], r4.at[k - 1], slab=lax.rem(slab + k, SLAB)
+        )
+
+    def send5(rel):
+        return remote(ag.at[own], ag.at[own], s5.at[0], r5.at[own], band=peer(rel))
+
+    def start5(rel, carry):
+        send5(rel).start()
+        return carry
+
+    @pl.when(owner)
+    def _():
+        out_row = iota((4 * WINDOW, 256), 0)
+        block = jnp.zeros(out_row.shape, jnp.int32)
+        for k in (1, 2, 3):
+            block = block + jnp.where(out_row >= k * WINDOW, 1, 0)
+        out_row = out_row - WINDOW * block
+        plane = jnp.where(out_row < CZ, out_row + CZ * block, -1)
+        source = iota((4 * WINDOW, 256), 1)
+        base = DEPTH * (source >> 4)
+        source = source & 15
+        gather = jnp.where(plane == base + source, 1.0, 0.0).astype(BF16)
+        tails = [
+            jnp.where(
+                jnp.logical_and(source >> 2 == c, plane == base + 16 + (source & 3)), 1.0, 0.0
+            ).astype(BF16)
+            for c in range(3)
+        ]
+        take(r3.at[0], rs3.at[pl.ds(0, BAND - 1)])
+        end = rs3[:, :, WIDE : WIDE + 128].reshape(256, 128)
+        whole = dot(gather, rs3[:, :, 0:WIDE].reshape(256, WIDE))
+        whole = whole + jnp.concatenate([dot(tails[c], end) for c in range(3)], axis=1)
+        for k in range(4):
+            st[k] = whole[k * WINDOW : (k + 1) * WINDOW]
+        for k in (1, 2, 3):
+            send4(k).start()
+
     sums = jnp.zeros((ATOMS, ROWS), F32)
     for d in range(DEPTH):
-        sums = sums + dot_nt(boxes[d], tables[d])
+        for c in range(TILES // 2):
+            sums = sums + dot_nt(boxes[d, :, 256 * c : 256 * c + 256], rows_of(tables, d, c))
     folded = jnp.zeros((ATOMS, 256), F32)
     for part in split(jnp.where(mine, sums, 0.0), 3):
         folded = folded + dot_nt(part, to_rows)
@@ -291,7 +339,7 @@
 
     def send6(rel):
         other = peer(rel)
-        return remote(isnd.at[other], ircv.at[me], s6.at[rel], r6.at[me], band=other)
+        return remote(isnd.at[other], ircv.at[me], s6.at[0], r6.at[0], band=other)
 
     def start6(rel, carry):
         send6(rel).start()
@@ -300,39 +348,8 @@
     lax.fori_loop(1, BAND, start6, 0)
     ircv[me] = isnd[me]
 
-    mark = (3 * me + 7) // 8
-    owner = jnp.logical_and(mark < OWNERS, 8 * mark // 3 == me)
-    own = jnp.minimum(mark, OWNERS - 1)
-
-    def wait3(rel, carry):
-        other = peer(rel)
-        remote(ext.at[0], rs3.at[other], s3.at[0], r3.at[other], band=other).wait_recv()
-        return carry
-
-    def send4(k):
-        return remote(
-            st.at[k], p4.at[k - 1], s4.at[k - 1], r4.at[k - 1], slab=lax.rem(slab + k, SLAB)
-        )
-
-    def send5(rel):
-        return remote(ag.at[own], ag.at[own], s5.at[rel], r5.at[own], band=peer(rel))
-
-    def start5(rel, carry):
-        send5(rel).start()
-        return carry
-
     @pl.when(owner)
     def _():
-        st[...] = jnp.zeros(st.shape, F32)
-        lax.fori_loop(1, BAND, wait3, 0)
-        for member in range(BAND):
-            k, row = divmod(member * DEPTH, CZ)
-            head = min(CZ - row, 20)
-            st[k, row : row + head, :] += rs3[member, 0:head, :]
-            if head < 20:
-                st[k + 1, 0 : 20 - head, :] += rs3[member, head:20, :]
-        for k in (1, 2, 3):
-            send4(k).start()
         for k in (1, 2, 3):
             send4(k).wait_recv()
         total = st[0] + p4[0] + p4[1] + p4[2]
@@ -344,12 +361,7 @@
         ag[own, :, WIDE : WIDE + 128] = exq[...].astype(BF16)
         lax.fori_loop(1, BAND, start5, 0)
 
-    def wait6(rel, carry):
-        other = peer(rel)
-        remote(isnd.at[0], ircv.at[other], s6.at[0], r6.at[other], band=other).wait_recv()
-        return carry
-
-    lax.fori_loop(1, BAND, wait6, 0)
+    take(r6.at[0], ircv.at[pl.ds(0, BAND - 1)])
     ints[...] = jnp.sum(ircv[...], axis=0)[:, 0:NPAIR]
 
     for j in range(OWNERS):
@@ -375,39 +387,27 @@
 
     send_pot(1).wait_send()
 
-    def end2(rel, carry):
-        send2(rel).wait_send()
-        return carry
-
     @pl.when(lax.rem(me, 4) == 0)
     def _():
-        lax.fori_loop(1, BAND, end2, 0)
+        take(s2.at[0], rs1.at[pl.ds(0, BAND - 1)])
 
     for j in range(OWNERS):
         @pl.when(me != 8 * j // 3)
         def _(j=j):
             send3(j).wait_send()
 
-    def end6(rel, carry):
-        send6(rel).wait_send()
-        return carry
-
-    lax.fori_loop(1, BAND, end6, 0)
-
-    def end5(rel, carry):
-        send5(rel).wait_send()
-        return carry
+    take(s6.at[0], ircv.at[pl.ds(0, BAND - 1)])
 
     @pl.when(owner)
     def _():
         for k in (1, 2, 3):
             send4(k).wait_send()
-        lax.fori_loop(1, BAND, end5, 0)
+        take(s5.at[0], rs3.at[pl.ds(0, BAND - 1)])
 
 
 def shards(projections, occupation, augment_tables, box_root, box_xy, species, potential):
     pt = jnp.transpose(projections, (1, 2, 0)).reshape(NH * ATOMS, 256)
-    tab = jnp.transpose(augment_tables, (1, 2, 0, 3))
+    tab = jnp.transpose(augment_tables.reshape(2, NPAIR, DEPTH, TILES, 128), (1, 2, 3, 0, 4))
     vmem = pl.BlockSpec(memory_space=pltpu.VMEM)
     dma = pltpu.SemaphoreType.DMA
     density, integrals = pl.pallas_call(
@@ -425,8 +425,7 @@
             pltpu.VMEM((1, ATOMS), jnp.int32),
             pltpu.VMEM((1, ATOMS), jnp.int32),
             pltpu.VMEM((CZ, GXY), F32),
-            pltpu.VMEM((PAD_P, DEPTH, 2, GXY), BF16),
-            pltpu.VMEM((DEPTH, ROWS, GXY), BF16),
+            pltpu.VMEM((DEPTH, TILES, PAD_P, 2, 128), BF16),
             pltpu.VMEM((4, 8, 128), F32),
             pltpu.VMEM((BAND, 8, 128), F32),
             pltpu.VMEM((4, 8, 128), F32),
@@ -434,8 +433,8 @@
             pltpu.VMEM((16, GXY + 384), BF16),
             pltpu.VMEM((2, 16, GXY + 384), BF16),
             pltpu.VMEM((DEPTH, ATOMS, GXY), BF16),
-            pltpu.VMEM((OWNERS, WINDOW, WIDE), F32),
-            pltpu.VMEM((BAND, WINDOW, WIDE), F32),
+            pltpu.VMEM((OWNERS, 16, WIDE + 128), BF16),
+            pltpu.VMEM((BAND, 16, WIDE + 128), BF16),
             pltpu.VMEM((4, WINDOW, WIDE), F32),
             pltpu.VMEM((3, WINDOW, WIDE), F32),
             pltpu.VMEM((16, 128), F32),
@@ -443,14 +442,14 @@
             pltpu.VMEM((ATOMS, 1, 256), F32),
             pltpu.VMEM((BAND, 1, 256), F32),
             dma((6,)),
-            dma,
-            dma((4,)), dma((BAND,)),
-            dma((BAND,)), dma((4,)),
+            dma((DEPTH,)),
+            dma((4,)), dma((1,)),
+            dma((1,)), dma((4,)),
             dma((2,)), dma((2,)),
-            dma((OWNERS,)), dma((BAND,)),
+            dma((OWNERS,)), dma((1,)),
             dma((3,)), dma((3,)),
-            dma((BAND,)), dma((OWNERS,)),
-            dma((BAND,)), dma((BAND,)),
+            dma((1,)), dma((OWNERS,)),
+            dma((1,)), dma((1,)),
         ],
         compiler_params=pltpu.CompilerParams(
             collective_id=0, has_side_effects=True, vmem_limit_bytes=56 << 20

time: 52.4 us -> 50 us (0.954)
  Pallas kernels: 48.8 us -> 46.4 us
    pallas_call x1, Pallas kernels: 48.8 us -> 46.4 us  [shards(): pl.pallas_call(kernel, out_shape=(jax.ShapeDtypeStruct((CZ, GXY), F32), j...]
where the time goes in v3:
time: 50 us; the launch traced here: 49.8 us
  Pallas kernels  46.4 us (93%)
  local copies, waits for them, and re-layouts  2.83 us (6%)
  between operations  0.64 us (1%)
    pallas_call x1, Pallas kernels, shards(): pl.pallas_call(kernel, out_shape=(jax.ShapeDtypeStruct((CZ, GXY), F32), j...  46.4 us
    unnamed x2, local copies, waits for them, and re-layouts  2.83 us

profile of v3, /device:TPU:1, one launch (start us, length us, event | category | flops | bytes accessed | tf_op | source)
XLA Modules:
  0.0 49.8 jit_solution(5843603724637034415)
XLA Ops:
  0.6 46.4 %shard_map.86 = (f32[18,2304]{1,0:T(8,128)}, f32[1,171]{1,0:T(1,128)}) custom-call(bf16[288,256]{1,0:T(8,128)(2,1)} %bitcast.12, f32[1,256]{1,0:T(1,128)} %bitcast.14, s32[1,16]{1,0:T(1,128)} %bitcast.15, s32[1,16]{1,0:T(1,128)} %bitcast.16, s32[1,16]{1,0:T(1,128)} %bitcast.17, f32[18,2304]{1,0:T(8,128)} %pot_hbm.1, bf16[171,3,18,2,128]{4,3,2,1,0:T(2,128)(2,1)} %bitcast.11), custom_call_target="tpu_custom_call" | custom-call | tf_op jit(solution)/shard_map/pallas_call | solution.py:413
  47.0 1.6 %copy.11 = f32[18,2304]{1,0:T(8,128)} copy(f32[18,2304]{1,0:T(8,128)} %get-tuple-element.8) | data formatting | bytes 331776
  48.6 1.2 %copy.12 = f32[171,1]{0,1:T(1,128)} copy(f32[171,1]{0,1:T(1,128)} %bitcast.13) | data formatting | bytes 1368

commit v4 on v3

--- a/solution.py
+++ b/solution.py
@@ -61,13 +61,46 @@
     pltpu.make_async_copy(landed, landed, sem).wait()
 
 
-def rotate(values, amount, left):
-    amount = jnp.broadcast_to(amount, values.shape)
-    for bit in range(12):
-        step = 1 << bit
-        turned = pltpu.roll(values, GXY - step if left else step, 1)
-        values = jnp.where((amount & step) != 0, turned, values)
-    return values
+def rotate(values, anchors, corners, left):
+    lane = iota((8, 128), 1)
+
+    def turn(v, step):
+        back = GXY - step if left else step
+        back = back % 128
+        turned = [pltpu.roll(x, back, 1) for x in v]
+        if left:
+            return [jnp.where(lane < back, turned[c], turned[(c + 1) % TILES]) for c in range(TILES)]
+        return [jnp.where(lane >= back, turned[c], turned[c - 1]) for c in range(TILES)]
+
+    def eight_rows(i, carry):
+        rows = pl.ds(pl.multiple_of(8 * i, 8), 8)
+        amount = anchors[rows, :]
+        v = [values[rows, 128 * c : 128 * c + 128] for c in range(TILES)]
+        for bit in range(12):
+            on = (amount & (1 << bit)) != 0
+            if bit < 7:
+                moved = turn(v, 1 << bit)
+            else:
+                hop = 1 << (bit - 7)
+                moved = [v[(c + hop if left else c - hop) % TILES] for c in range(TILES)]
+            v = [jnp.where(on, moved[c], v[c]) for c in range(TILES)]
+        corner = corners[rows, :]
+        inside = []
+        for c in range(3):
+            line = lane + 128 * c % GX
+            for end in (GX, 2 * GX, 3 * GX):
+                line = line - jnp.where(lane + 128 * c % GX >= end, GX, 0)
+            inside.append(line < GX - corner if left else line >= corner)
+        wrap = [pltpu.roll(x, GX if left else 128 - GX, 1) for x in v]
+        for c in range(TILES):
+            if left:
+                wrapped = jnp.where(lane >= GX, wrap[c], wrap[c - 1])
+            else:
+                wrapped = jnp.where(lane < 128 - GX, wrap[c], wrap[(c + 1) % TILES])
+            values[rows, 128 * c : 128 * c + 128] = jnp.where(inside[c % 3], v[c], wrapped)
+        return carry
+
+    lax.fori_loop(0, DEPTH * ATOMS // 8, eight_rows, 0)
 
 
 def remote(src, dst, send, recv, **where):
@@ -83,7 +116,7 @@
 
 def kernel(
     pt_hbm, occ_hbm, root_hbm, xy_hbm, kind_hbm, pot_hbm, tab, dens, ints,
-    pt, occ, root, xy, kind, pot, tables, bt, rs1, tt, pex, pout, pin, boxes, ext, rs3, st, p4, exq, ag, isnd, ircv,
+    pt, occ, root, xy, kind, pot, tables, bt, rs1, tt, pex, pout, pin, boxes, ext, rs3, st, p4, values, anchors, corners, ag, isnd, ircv,
     in_sem, tab_sem, s1, r1, s2, r2, sp, rp, s3, r3, s4, r4, s5, r5, s6, r6,
 ):
     me = lax.axis_index("band")
@@ -92,6 +125,14 @@
     def peer(rel):
         return lax.rem(me + rel, BAND)
 
+    loads = [
+        pltpu.make_async_copy(src, dst, in_sem.at[n])
+        for n, (src, dst) in enumerate(
+            [(pt_hbm, pt), (occ_hbm, occ), (pot_hbm, pot), (root_hbm, root), (xy_hbm, xy), (kind_hbm, kind)]
+        )
+    ]
+    loads[0].start()
+    loads[1].start()
     barrier = pltpu.get_barrier_semaphore()
 
     def greet(rel, carry):
@@ -106,20 +147,8 @@
             barrier, inc=1, device_id={"slab": lax.rem(slab + k, SLAB)},
             device_id_type=pl.DeviceIdType.MESH,
         )
-    loads = [
-        pltpu.make_async_copy(src, dst, in_sem.at[n])
-        for n, (src, dst) in enumerate(
-            [(pt_hbm, pt), (occ_hbm, occ), (pot_hbm, pot), (root_hbm, root), (xy_hbm, xy), (kind_hbm, kind)]
-        )
-    ]
-    for load in loads:
+    for load in loads[2:]:
         load.start()
-    tables[:, :, NPAIR:PAD_P] = jnp.zeros((DEPTH, TILES, PAD_P - NPAIR, 2, 128), BF16)
-    for d in range(DEPTH):
-        for c in range(TILES):
-            pltpu.make_async_copy(
-                tab.at[:, d, c], tables.at[d, c, pl.ds(0, NPAIR)], tab_sem.at[d]
-            ).start()
 
     size = NH * ATOMS
     same = (iota((size, size), 0) & 15) == (iota((size, size), 1) & 15)
@@ -134,6 +163,12 @@
     pick_j = jnp.where((iota((size, 256), 0) >> 4) == j_of, 1.0, 0.0).astype(BF16)
     loads[0].wait()
     loads[1].wait()
+    tables[:, :, NPAIR:PAD_P] = jnp.zeros((DEPTH, TILES, PAD_P - NPAIR, 2, 128), BF16)
+    for d in range(DEPTH):
+        for c in range(TILES):
+            pltpu.make_async_copy(
+                tab.at[:, d, c], tables.at[d, c, pl.ds(0, NPAIR)], tab_sem.at[d]
+            ).start()
     p = pt[...]
     weighted = split(p.astype(F32) * occ[...], 2)
     gram = dot_nt(weighted[0], p) + dot_nt(weighted[1], p)
@@ -213,9 +248,9 @@
     anchor = column(xy[...])
     species = column(kind[...])
     corner = anchor - GX * ((anchor.astype(F32) + 0.5) * (1.0 / GX)).astype(jnp.int32)
-    lane = iota((ATOMS, GXY), 1)
-    line = lane - GX * ((lane.astype(F32) + 0.5) * (1.0 / GX)).astype(jnp.int32)
-    corner = jnp.broadcast_to(corner, (ATOMS, GXY))
+    for d in range(DEPTH):
+        anchors[d * ATOMS : (d + 1) * ATOMS, :] = jnp.broadcast_to(anchor, (ATOMS, 128))
+        corners[d * ATOMS : (d + 1) * ATOMS, :] = jnp.broadcast_to(corner, (ATOMS, 128))
     mine = jnp.broadcast_to(species, (ATOMS, ROWS)) == (iota((ATOMS, ROWS), 1) & 1)
     to_rows = jnp.where((iota((256, ROWS), 1) >> 1) == iota((256, ROWS), 0), 1.0, 0.0).astype(BF16)
 
@@ -232,13 +267,15 @@
         axis=0,
     ).astype(BF16)
     left = jnp.where(mine, dot(packed, to_rows), 0.0).astype(BF16)
+    for d in range(DEPTH):
+        terms = [dot(left, rows_of(tables, d, c)) for c in range(TILES // 2)]
+        for c in range(TILES // 2):
+            values[d * ATOMS : (d + 1) * ATOMS, 256 * c : 256 * c + 256] = terms[c]
+    rotate(values, anchors, corners, False)
     window = jnp.zeros((WINDOW, GXY), F32)
     for d in range(DEPTH):
-        terms = [dot(left, rows_of(tables, d, c)) for c in range(TILES // 2)]
-        placed = rotate(jnp.concatenate(terms, axis=1), anchor, False)
-        placed = jnp.where(line >= corner, placed, pltpu.roll(placed, GXY - GX, 1))
         onto = jnp.where(iota((WINDOW, ATOMS), 0) == offset_row + d, 1.0, 0.0).astype(BF16)
-        for part in split(placed, 2):
+        for part in split(values[d * ATOMS : (d + 1) * ATOMS, :], 2):
             window = window + dot(onto, part)
     for j in range(OWNERS):
         ext[j, :, 0:WIDE] = window[0:16, j * WIDE : (j + 1) * WIDE].astype(BF16)
@@ -280,9 +317,10 @@
         choose = jnp.where(
             iota((ATOMS, 48), 1) == jnp.broadcast_to(source, (ATOMS, 48)), 1.0, 0.0
         ).astype(BF16)
-        turned = rotate(dot(choose, planes), anchor, True)
-        turned = jnp.where(line < GX - corner, turned, pltpu.roll(turned, GX, 1))
-        boxes[d] = turned.astype(BF16)
+        values[d * ATOMS : (d + 1) * ATOMS, :] = dot(choose, planes)
+    rotate(values, anchors, corners, True)
+    for d in range(DEPTH):
+        boxes[d] = values[d * ATOMS : (d + 1) * ATOMS, :].astype(BF16)
 
     mark = (3 * me + 7) // 8
     owner = jnp.logical_and(mark < OWNERS, 8 * mark // 3 == me)
@@ -345,36 +383,36 @@
         send6(rel).start()
         return carry
 
-    lax.fori_loop(1, BAND, start6, 0)
-    ircv[me] = isnd[me]
-
     @pl.when(owner)
     def _():
         for k in (1, 2, 3):
             send4(k).wait_recv()
         total = st[0] + p4[0] + p4[1] + p4[2]
-        exq[...] = jnp.zeros(exq.shape, F32)
-        for r in range(2):
-            for c in range(3):
-                exq[r * 3 + c : r * 3 + c + 1, :] = total[16 + r : 17 + r, c * 128 : c * 128 + 128]
+        ends = [total[16:24, c * 128 : c * 128 + 128] for c in range(3)]
+        ends = ends[0] + pltpu.roll(ends[1], 2, 0) + pltpu.roll(ends[2], 4, 0)
+        ends = jnp.concatenate([ends, jnp.zeros_like(ends)], axis=0)
         ag[own, :, 0:WIDE] = total[0:16].astype(BF16)
-        ag[own, :, WIDE : WIDE + 128] = exq[...].astype(BF16)
+        ag[own, :, WIDE : WIDE + 128] = ends.astype(BF16)
         lax.fori_loop(1, BAND, start5, 0)
 
+    lax.fori_loop(1, BAND, start6, 0)
+    ircv[me] = isnd[me]
+
     take(r6.at[0], ircv.at[pl.ds(0, BAND - 1)])
-    ints[...] = jnp.sum(ircv[...], axis=0)[:, 0:NPAIR]
+    ints[...] = jnp.sum(ircv[...], axis=0)
 
     for j in range(OWNERS):
         @pl.when(me != 8 * j // 3)
         def _(j=j):
             remote(ag.at[j], ag.at[j], s5.at[0], r5.at[j], band=8 * j // 3).wait_recv()
 
-        dens[0:16, j * WIDE : (j + 1) * WIDE] = ag[j, :, 0:WIDE].astype(F32)
-        tail = ag[j, :, WIDE : WIDE + 128].astype(F32)
-        for r in range(2):
-            for c in range(3):
-                at = j * WIDE + c * 128
-                dens[16 + r : 17 + r, at : at + 128] = tail[r * 3 + c : r * 3 + c + 1]
+        dens[0:16, j * WIDE : (j + 1) * WIDE] = ag[j, :, 0:WIDE]
+        ends = ag[j, :, WIDE : WIDE + 128].astype(F32)[0:8]
+        for c in range(3):
+            at = j * WIDE + c * 128
+            tail = pltpu.roll(ends, 8 - 2 * c, 0) if c else ends
+            tail = jnp.concatenate([tail, jnp.zeros_like(tail)], axis=0)
+            dens[16:32, at : at + 128] = tail.astype(BF16)
 
     for t in range(4):
         @pl.when(me != 4 * t)
@@ -413,8 +451,8 @@
     density, integrals = pl.pallas_call(
         kernel,
         out_shape=(
-            jax.ShapeDtypeStruct((CZ, GXY), F32),
-            jax.ShapeDtypeStruct((1, NPAIR), F32),
+            jax.ShapeDtypeStruct((32, GXY), BF16),
+            jax.ShapeDtypeStruct((1, 256), F32),
         ),
         in_specs=[pl.BlockSpec(memory_space=pltpu.HBM)] * 7,
         out_specs=(vmem, vmem),
@@ -437,7 +475,9 @@
             pltpu.VMEM((BAND, 16, WIDE + 128), BF16),
             pltpu.VMEM((4, WINDOW, WIDE), F32),
             pltpu.VMEM((3, WINDOW, WIDE), F32),
-            pltpu.VMEM((16, 128), F32),
+            pltpu.VMEM((DEPTH * ATOMS, GXY), F32),
+            pltpu.VMEM((DEPTH * ATOMS, 128), jnp.int32),
+            pltpu.VMEM((DEPTH * ATOMS, 128), jnp.int32),
             pltpu.VMEM((OWNERS, 16, WIDE + 128), BF16),
             pltpu.VMEM((ATOMS, 1, 256), F32),
             pltpu.VMEM((BAND, 1, 256), F32),
@@ -463,7 +503,7 @@
         potential,
         tab,
     )
-    return density, integrals.reshape(NPAIR, 1)
+    return density[0:CZ].astype(F32), integrals[:, 0:NPAIR].reshape(NPAIR, 1)
 
 
 def solution(mesh):

time: 50 us -> 52.6 us (1.052)
  Pallas kernels: 46.4 us -> 49 us
  local copies, waits for them, and re-layouts: 2.83 us -> 1.22 us
  other arithmetic: 0 us -> 1.6 us
    unnamed x2 -> x0, local copies, waits for them, and re-layouts: 2.83 us -> none
    pallas_call x1, Pallas kernels: 46.4 us -> 49 us  [shards(): pl.pallas_call(kernel, out_shape=(jax.ShapeDtypeStruct((32, GXY), BF16),...]
    convert_element_type x0 -> x1, other arithmetic: none -> 1.6 us  [shards(): return (density[0:CZ].astype(F32), integrals[:, 0:NPAIR].reshape(NPAIR, 1))]
    reshape x0 -> x1, local copies, waits for them, and re-layouts: none -> 1.22 us  [shards(): return (density[0:CZ].astype(F32), integrals[:, 0:NPAIR].reshape(NPAIR, 1))]
where the time goes in v4:
time: 52.6 us; the launch traced here: 52.5 us
  Pallas kernels  49 us (93%)
  other arithmetic  1.6 us (3%)
  local copies, waits for them, and re-layouts  1.22 us (2%)
  between operations  0.64 us (1%)
    pallas_call x1, Pallas kernels, shards(): pl.pallas_call(kernel, out_shape=(jax.ShapeDtypeStruct((32, GXY), BF16),...  49 us
    convert_element_type x1, other arithmetic, shards(): return (density[0:CZ].astype(F32), integrals[:, 0:NPAIR].reshape(NPAIR, 1))  1.6 us
    reshape x1, local copies, waits for them, and re-layouts, shards(): return (density[0:CZ].astype(F32), integrals[:, 0:NPAIR].reshape(NPAIR, 1))  1.22 us

profile of v4, /device:TPU:1, one launch (start us, length us, event | category | flops | bytes accessed | tf_op | source)
XLA Modules:
  0.0 52.5 jit_solution(6990250070266043672)
XLA Ops:
  0.6 49.0 %shard_map.86 = (bf16[32,2304]{1,0:T(8,128)(2,1)}, f32[1,256]{1,0:T(1,128)}) custom-call(bf16[288,256]{1,0:T(8,128)(2,1)} %bitcast.13, f32[1,256]{1,0:T(1,128)} %bitcast.14, s32[1,16]{1,0:T(1,128)} %bitcast.15, s32[1,16]{1,0:T(1,128)} %bitcast.16, s32[1,16]{1,0:T(1,128)} %bitcast.17, f32[18,2304]{1,0:T(8,128)} %pot_hbm.1, bf16[171,3,18,2,128]{4,3,2,1,0:T(2,128)(2,1)} %bitcast.12), custom_call_target="tpu_custom_call" | custom-call | tf_op jit(solution)/shard_map/pallas_call | solution.py:451
  49.7 1.2 %slice_bitcast_fusion = f32[171,1]{0,1:T(1,128)} fusion(f32[1,256]{1,0:T(1,128)} %get-tuple-element.5), kind=kLoop, calls=%fused_computation.1 | loop fusion | bytes 1368 | tf_op jit(solution)/shard_map/reshape | solution.py:506
  50.9 1.6 %slice_convert_fusion = f32[18,2304]{1,0:T(8,128)} fusion(bf16[32,2304]{1,0:T(8,128)(2,1)} %get-tuple-element.4), kind=kLoop, calls=%fused_computation | loop fusion | flops 41472 | bytes 248832 | tf_op jit(solution)/shard_map/convert_element_type | solution.py:506

commit v5 on v4

--- a/solution.py
+++ b/solution.py
@@ -20,6 +20,8 @@
 WIDE = GXY // OWNERS
 WINDOW = 24
 TILES = 18
+SPREAD = 6
+EARLY = 8
 F32 = jnp.float32
 BF16 = jnp.bfloat16
 NT = (((1,), (1,)), ((), ()))
@@ -116,8 +118,8 @@
 
 def kernel(
     pt_hbm, occ_hbm, root_hbm, xy_hbm, kind_hbm, pot_hbm, tab, dens, ints,
-    pt, occ, root, xy, kind, pot, tables, bt, rs1, tt, pex, pout, pin, boxes, ext, rs3, st, p4, values, anchors, corners, ag, isnd, ircv,
-    in_sem, tab_sem, s1, r1, s2, r2, sp, rp, s3, r3, s4, r4, s5, r5, s6, r6,
+    pt, occ, root, xy, kind, pot, raw, tables, bt, rs1, tt, pex, pout, pin, boxes, ext, rs3, st, p4, values, anchors, corners, ag, isnd, ircv,
+    in_sem, raw_sem, tab_sem, s1, r1, s2, r2, sp, rp, s3, r3, s4, r4, s5, r5, s6, r6,
 ):
     me = lax.axis_index("band")
     slab = lax.axis_index("slab")
@@ -149,6 +151,15 @@
         )
     for load in loads[2:]:
         load.start()
+    whole = pltpu.make_async_copy(tab.at[:, :, pl.ds(SPREAD, TILES - SPREAD)], raw.at[pl.ds(0, NPAIR)], raw_sem)
+    whole.start()
+    for d in range(DEPTH):
+        for c in range(SPREAD):
+            pltpu.make_async_copy(
+                tab.at[:, d, c], tables.at[d, c, pl.ds(0, NPAIR)], tab_sem.at[d]
+            ).start()
+    tables[:, 0:SPREAD, NPAIR:PAD_P] = jnp.zeros((DEPTH, SPREAD, PAD_P - NPAIR, 2, 128), BF16)
+    raw[NPAIR:PAD_P] = jnp.zeros((PAD_P - NPAIR, DEPTH, TILES - SPREAD, 2, 128), BF16)
 
     size = NH * ATOMS
     same = (iota((size, size), 0) & 15) == (iota((size, size), 1) & 15)
@@ -163,12 +174,6 @@
     pick_j = jnp.where((iota((size, 256), 0) >> 4) == j_of, 1.0, 0.0).astype(BF16)
     loads[0].wait()
     loads[1].wait()
-    tables[:, :, NPAIR:PAD_P] = jnp.zeros((DEPTH, TILES, PAD_P - NPAIR, 2, 128), BF16)
-    for d in range(DEPTH):
-        for c in range(TILES):
-            pltpu.make_async_copy(
-                tab.at[:, d, c], tables.at[d, c, pl.ds(0, NPAIR)], tab_sem.at[d]
-            ).start()
     p = pt[...]
     weighted = split(p.astype(F32) * occ[...], 2)
     gram = dot_nt(weighted[0], p) + dot_nt(weighted[1], p)
@@ -222,6 +227,15 @@
 
     send_pot(1).start()
 
+    def regroup(n, carry):
+        for d in range(DEPTH):
+            for c in range(TILES - SPREAD):
+                tables[d, SPREAD + c, pl.ds(8 * n, 8)] = raw[pl.ds(8 * n, 8), d, c]
+        return carry
+
+    whole.wait()
+    lax.fori_loop(0, EARLY, regroup, 0)
+
     tile = me // 4
 
     def send2(rel):
@@ -237,8 +251,9 @@
         tt[tile] = jnp.sum(rs1[...], axis=0)
         lax.fori_loop(1, BAND, start2, 0)
 
-    for d in range(DEPTH):
-        part = tables.at[d, :, pl.ds(0, NPAIR)]
+    lax.fori_loop(EARLY, PAD_P // 8, regroup, 0)
+    for d in range(DEPTH):
+        part = tables.at[d, pl.ds(0, SPREAD), pl.ds(0, NPAIR)]
         pltpu.make_async_copy(part, part, tab_sem.at[d]).wait()
     for load in loads[3:]:
         load.wait()
@@ -358,10 +373,10 @@
         ]
         take(r3.at[0], rs3.at[pl.ds(0, BAND - 1)])
         end = rs3[:, :, WIDE : WIDE + 128].reshape(256, 128)
-        whole = dot(gather, rs3[:, :, 0:WIDE].reshape(256, WIDE))
-        whole = whole + jnp.concatenate([dot(tails[c], end) for c in range(3)], axis=1)
+        summed = dot(gather, rs3[:, :, 0:WIDE].reshape(256, WIDE))
+        summed = summed + jnp.concatenate([dot(tails[c], end) for c in range(3)], axis=1)
         for k in range(4):
-            st[k] = whole[k * WINDOW : (k + 1) * WINDOW]
+            st[k] = summed[k * WINDOW : (k + 1) * WINDOW]
         for k in (1, 2, 3):
             send4(k).start()
 
@@ -463,6 +478,7 @@
             pltpu.VMEM((1, ATOMS), jnp.int32),
             pltpu.VMEM((1, ATOMS), jnp.int32),
             pltpu.VMEM((CZ, GXY), F32),
+            pltpu.VMEM((PAD_P, DEPTH, TILES - SPREAD, 2, 128), BF16),
             pltpu.VMEM((DEPTH, TILES, PAD_P, 2, 128), BF16),
             pltpu.VMEM((4, 8, 128), F32),
             pltpu.VMEM((BAND, 8, 128), F32),
@@ -482,6 +498,7 @@
             pltpu.VMEM((ATOMS, 1, 256), F32),
             pltpu.VMEM((BAND, 1, 256), F32),
             dma((6,)),
+            dma,
             dma((DEPTH,)),
             dma((4,)), dma((1,)),
             dma((1,)), dma((4,)),

time: 52.6 us -> 52.6 us (level)
  no operation moved by 1% of the time
where the time goes in v5:
time: 52.6 us; the launch traced here: 52.5 us
  Pallas kernels  49 us (93%)
  other arithmetic  1.6 us (3%)
  local copies, waits for them, and re-layouts  1.22 us (2%)
  between operations  0.64 us (1%)
    pallas_call x1, Pallas kernels, shards(): pl.pallas_call(kernel, out_shape=(jax.ShapeDtypeStruct((32, GXY), BF16),...  49 us
    convert_element_type x1, other arithmetic, shards(): return (density[0:CZ].astype(F32), integrals[:, 0:NPAIR].reshape(NPAIR, 1))  1.6 us
    reshape x1, local copies, waits for them, and re-layouts, shards(): return (density[0:CZ].astype(F32), integrals[:, 0:NPAIR].reshape(NPAIR, 1))  1.22 us

profile of v5, /device:TPU:1, one launch (start us, length us, event | category | flops | bytes accessed | tf_op | source)
XLA Modules:
  0.0 52.5 jit_solution(807471391828882338)
XLA Ops:
  0.6 49.0 %shard_map.86 = (bf16[32,2304]{1,0:T(8,128)(2,1)}, f32[1,256]{1,0:T(1,128)}) custom-call(bf16[288,256]{1,0:T(8,128)(2,1)} %bitcast.13, f32[1,256]{1,0:T(1,128)} %bitcast.14, s32[1,16]{1,0:T(1,128)} %bitcast.15, s32[1,16]{1,0:T(1,128)} %bitcast.16, s32[1,16]{1,0:T(1,128)} %bitcast.17, f32[18,2304]{1,0:T(8,128)} %pot_hbm.1, bf16[171,3,18,2,128]{4,3,2,1,0:T(2,128)(2,1)} %bitcast.12), custom_call_target="tpu_custom_call" | custom-call | tf_op jit(solution)/shard_map/pallas_call | solution.py:466
  49.7 1.2 %slice_bitcast_fusion = f32[171,1]{0,1:T(1,128)} fusion(f32[1,256]{1,0:T(1,128)} %get-tuple-element.5), kind=kLoop, calls=%fused_computation.1 | loop fusion | bytes 1368 | tf_op jit(solution)/shard_map/reshape | solution.py:523
  50.9 1.6 %slice_convert_fusion = f32[18,2304]{1,0:T(8,128)} fusion(bf16[32,2304]{1,0:T(8,128)(2,1)} %get-tuple-element.4), kind=kLoop, calls=%fused_computation | loop fusion | flops 41472 | bytes 248832 | tf_op jit(solution)/shard_map/convert_element_type | solution.py:523

commit v6 on v3

--- a/solution.py
+++ b/solution.py
@@ -83,7 +83,7 @@
 
 def kernel(
     pt_hbm, occ_hbm, root_hbm, xy_hbm, kind_hbm, pot_hbm, tab, dens, ints,
-    pt, occ, root, xy, kind, pot, tables, bt, rs1, tt, pex, pout, pin, boxes, ext, rs3, st, p4, exq, ag, isnd, ircv,
+    pt, occ, root, xy, kind, pot, tables, bt, rs1, tt, pex, pout, pin, boxes, ext, rs3, st, p4, ag, isnd, ircv,
     in_sem, tab_sem, s1, r1, s2, r2, sp, rp, s3, r3, s4, r4, s5, r5, s6, r6,
 ):
     me = lax.axis_index("band")
@@ -92,6 +92,14 @@
     def peer(rel):
         return lax.rem(me + rel, BAND)
 
+    loads = [
+        pltpu.make_async_copy(src, dst, in_sem.at[n])
+        for n, (src, dst) in enumerate(
+            [(pt_hbm, pt), (occ_hbm, occ), (pot_hbm, pot), (root_hbm, root), (xy_hbm, xy), (kind_hbm, kind)]
+        )
+    ]
+    loads[0].start()
+    loads[1].start()
     barrier = pltpu.get_barrier_semaphore()
 
     def greet(rel, carry):
@@ -106,13 +114,7 @@
             barrier, inc=1, device_id={"slab": lax.rem(slab + k, SLAB)},
             device_id_type=pl.DeviceIdType.MESH,
         )
-    loads = [
-        pltpu.make_async_copy(src, dst, in_sem.at[n])
-        for n, (src, dst) in enumerate(
-            [(pt_hbm, pt), (occ_hbm, occ), (pot_hbm, pot), (root_hbm, root), (xy_hbm, xy), (kind_hbm, kind)]
-        )
-    ]
-    for load in loads:
+    for load in loads[2:]:
         load.start()
     tables[:, :, NPAIR:PAD_P] = jnp.zeros((DEPTH, TILES, PAD_P - NPAIR, 2, 128), BF16)
     for d in range(DEPTH):
@@ -213,9 +215,10 @@
     anchor = column(xy[...])
     species = column(kind[...])
     corner = anchor - GX * ((anchor.astype(F32) + 0.5) * (1.0 / GX)).astype(jnp.int32)
-    lane = iota((ATOMS, GXY), 1)
+    lane = iota((DEPTH * ATOMS, GXY), 1)
     line = lane - GX * ((lane.astype(F32) + 0.5) * (1.0 / GX)).astype(jnp.int32)
-    corner = jnp.broadcast_to(corner, (ATOMS, GXY))
+    corner = jnp.broadcast_to(jnp.concatenate([corner] * DEPTH, axis=0), line.shape)
+    anchor = jnp.concatenate([anchor] * DEPTH, axis=0)
     mine = jnp.broadcast_to(species, (ATOMS, ROWS)) == (iota((ATOMS, ROWS), 1) & 1)
     to_rows = jnp.where((iota((256, ROWS), 1) >> 1) == iota((256, ROWS), 0), 1.0, 0.0).astype(BF16)
 
@@ -232,14 +235,19 @@
         axis=0,
     ).astype(BF16)
     left = jnp.where(mine, dot(packed, to_rows), 0.0).astype(BF16)
+    terms = []
+    for d in range(DEPTH):
+        terms.append(
+            jnp.concatenate([dot(left, rows_of(tables, d, c)) for c in range(TILES // 2)], axis=1)
+        )
+    placed = rotate(jnp.concatenate(terms, axis=0), anchor, False)
+    placed = jnp.where(line >= corner, placed, pltpu.roll(placed, GXY - GX, 1))
+    parts = split(placed, 2)
     window = jnp.zeros((WINDOW, GXY), F32)
     for d in range(DEPTH):
-        terms = [dot(left, rows_of(tables, d, c)) for c in range(TILES // 2)]
-        placed = rotate(jnp.concatenate(terms, axis=1), anchor, False)
-        placed = jnp.where(line >= corner, placed, pltpu.roll(placed, GXY - GX, 1))
         onto = jnp.where(iota((WINDOW, ATOMS), 0) == offset_row + d, 1.0, 0.0).astype(BF16)
-        for part in split(placed, 2):
-            window = window + dot(onto, part)
+        for part in parts:
+            window = window + dot(onto, part[d * ATOMS : (d + 1) * ATOMS])
     for j in range(OWNERS):
         ext[j, :, 0:WIDE] = window[0:16, j * WIDE : (j + 1) * WIDE].astype(BF16)
         ends = [window[16:24, j * WIDE + c * 128 : j * WIDE + c * 128 + 128] for c in range(3)]
@@ -272,6 +280,7 @@
             )
     extra = jnp.concatenate(extra + [jnp.zeros((12, GXY), F32)], axis=0).astype(BF16)
     planes = jnp.concatenate([pin[0, :, 0:GXY], pin[1, :, 0:GXY], extra], axis=0)
+    picked = []
     for d in range(DEPTH):
         target = offset + (first + d)
         late = jnp.where(target >= CZ, 1, 0)
@@ -280,9 +289,11 @@
         choose = jnp.where(
             iota((ATOMS, 48), 1) == jnp.broadcast_to(source, (ATOMS, 48)), 1.0, 0.0
         ).astype(BF16)
-        turned = rotate(dot(choose, planes), anchor, True)
-        turned = jnp.where(line < GX - corner, turned, pltpu.roll(turned, GX, 1))
-        boxes[d] = turned.astype(BF16)
+        picked.append(dot(choose, planes))
+    turned = rotate(jnp.concatenate(picked, axis=0), anchor, True)
+    turned = jnp.where(line < GX - corner, turned, pltpu.roll(turned, GX, 1))
+    for d in range(DEPTH):
+        boxes[d] = turned[d * ATOMS : (d + 1) * ATOMS].astype(BF16)
 
     mark = (3 * me + 7) // 8
     owner = jnp.logical_and(mark < OWNERS, 8 * mark // 3 == me)
@@ -353,28 +364,28 @@
         for k in (1, 2, 3):
             send4(k).wait_recv()
         total = st[0] + p4[0] + p4[1] + p4[2]
-        exq[...] = jnp.zeros(exq.shape, F32)
-        for r in range(2):
-            for c in range(3):
-                exq[r * 3 + c : r * 3 + c + 1, :] = total[16 + r : 17 + r, c * 128 : c * 128 + 128]
+        ends = [total[16:24, c * 128 : c * 128 + 128] for c in range(3)]
+        ends = ends[0] + pltpu.roll(ends[1], 2, 0) + pltpu.roll(ends[2], 4, 0)
+        ends = jnp.concatenate([ends, jnp.zeros_like(ends)], axis=0)
         ag[own, :, 0:WIDE] = total[0:16].astype(BF16)
-        ag[own, :, WIDE : WIDE + 128] = exq[...].astype(BF16)
+        ag[own, :, WIDE : WIDE + 128] = ends.astype(BF16)
         lax.fori_loop(1, BAND, start5, 0)
 
     take(r6.at[0], ircv.at[pl.ds(0, BAND - 1)])
-    ints[...] = jnp.sum(ircv[...], axis=0)[:, 0:NPAIR]
+    ints[...] = jnp.sum(ircv[...], axis=0)
 
     for j in range(OWNERS):
         @pl.when(me != 8 * j // 3)
         def _(j=j):
             remote(ag.at[j], ag.at[j], s5.at[0], r5.at[j], band=8 * j // 3).wait_recv()
 
-        dens[0:16, j * WIDE : (j + 1) * WIDE] = ag[j, :, 0:WIDE].astype(F32)
-        tail = ag[j, :, WIDE : WIDE + 128].astype(F32)
-        for r in range(2):
-            for c in range(3):
-                at = j * WIDE + c * 128
-                dens[16 + r : 17 + r, at : at + 128] = tail[r * 3 + c : r * 3 + c + 1]
+        dens[0:16, j * WIDE : (j + 1) * WIDE] = ag[j, :, 0:WIDE]
+        ends = ag[j, :, WIDE : WIDE + 128].astype(F32)[0:8]
+        for c in range(3):
+            at = j * WIDE + c * 128
+            tail = pltpu.roll(ends, 8 - 2 * c, 0) if c else ends
+            tail = jnp.concatenate([tail, jnp.zeros_like(tail)], axis=0)
+            dens[16:32, at : at + 128] = tail.astype(BF16)
 
     for t in range(4):
         @pl.when(me != 4 * t)
@@ -403,6 +414,11 @@
         for k in (1, 2, 3):
             send4(k).wait_send()
         take(s5.at[0], rs3.at[pl.ds(0, BAND - 1)])
+
+
+def finish(rounded, sums, density, integrals):
+    density[...] = rounded[...].astype(F32)[0:CZ]
+    integrals[...] = sums[:, 0:NPAIR]
 
 
 def shards(projections, occupation, augment_tables, box_root, box_xy, species, potential):
@@ -413,8 +429,8 @@
     density, integrals = pl.pallas_call(
         kernel,
         out_shape=(
-            jax.ShapeDtypeStruct((CZ, GXY), F32),
-            jax.ShapeDtypeStruct((1, NPAIR), F32),
+            jax.ShapeDtypeStruct((32, GXY), BF16),
+            jax.ShapeDtypeStruct((1, 256), F32),
         ),
         in_specs=[pl.BlockSpec(memory_space=pltpu.HBM)] * 7,
         out_specs=(vmem, vmem),
@@ -437,7 +453,6 @@
             pltpu.VMEM((BAND, 16, WIDE + 128), BF16),
             pltpu.VMEM((4, WINDOW, WIDE), F32),
             pltpu.VMEM((3, WINDOW, WIDE), F32),
-            pltpu.VMEM((16, 128), F32),
             pltpu.VMEM((OWNERS, 16, WIDE + 128), BF16),
             pltpu.VMEM((ATOMS, 1, 256), F32),
             pltpu.VMEM((BAND, 1, 256), F32),
@@ -463,6 +478,16 @@
         potential,
         tab,
     )
+    density, integrals = pl.pallas_call(
+        finish,
+        out_shape=(
+            jax.ShapeDtypeStruct((CZ, GXY), F32),
+            jax.ShapeDtypeStruct((1, NPAIR), F32),
+        ),
+        in_specs=[vmem] * 2,
+        out_specs=(vmem, vmem),
+        compiler_params=pltpu.CompilerParams(vmem_limit_bytes=56 << 20),
+    )(density, integrals)
     return density, integrals.reshape(NPAIR, 1)
 
 

time: 50 us -> 47.9 us (0.958)
  local copies, waits for them, and re-layouts: 2.83 us -> 0 us
  Pallas kernels: 46.4 us -> 47.1 us
    unnamed x2 -> x0, local copies, waits for them, and re-layouts: 2.83 us -> none
    pallas_call x1 -> x2, Pallas kernels: 46.4 us -> 47.1 us  [the longest x1 45.5 us: shards(): pl.pallas_call(kernel, out_shape=(jax.ShapeDtypeStruct((32, GXY), BF16),...]
where the time goes in v6:
time: 47.9 us; the launch traced here: 47.8 us
  Pallas kernels  47.1 us (98%)
  between operations  0.64 us (1%)
    pallas_call x1, Pallas kernels, shards(): pl.pallas_call(kernel, out_shape=(jax.ShapeDtypeStruct((32, GXY), BF16),...  45.5 us
    pallas_call x1, Pallas kernels, shards(): pl.pallas_call(finish, out_shape=(jax.ShapeDtypeStruct((CZ, GXY), F32), j...  1.62 us

profile of v6, /device:TPU:1, one launch (start us, length us, event | category | flops | bytes accessed | tf_op | source)
XLA Modules:
  0.0 47.8 jit_solution(7678838133293306739)
XLA Ops:
  0.6 45.5 %shard_map.86 = (bf16[32,2304]{1,0:T(8,128)(2,1)}, f32[1,256]{1,0:T(1,128)}) custom-call(bf16[288,256]{1,0:T(8,128)(2,1)} %bitcast.12, f32[1,256]{1,0:T(1,128)} %bitcast.13, s32[1,16]{1,0:T(1,128)} %bitcast.14, s32[1,16]{1,0:T(1,128)} %bitcast.15, s32[1,16]{1,0:T(1,128)} %bitcast.16, f32[18,2304]{1,0:T(8,128)} %pot_hbm.1, bf16[171,3,18,2,128]{4,3,2,1,0:T(2,128)(2,1)} %bitcast.11), custom_call_target="tpu_custom_call" | custom-call | tf_op jit(solution)/shard_map/pallas_call | solution.py:429
  46.2 1.6 %shard_map.87 = (f32[18,2304]{1,0:T(8,128)}, f32[1,171]{1,0:T(1,128)}) custom-call(bf16[32,2304]{1,0:T(8,128)(2,1)} %get-tuple-element.6.rounded, f32[1,256]{1,0:T(1,128)} %get-tuple-element.7.sums), custom_call_target="tpu_custom_call" | custom-call | tf_op jit(solution)/shard_map/pallas_call | solution.py:481

commit v7 on v6

--- a/solution.py
+++ b/solution.py
@@ -82,9 +82,9 @@
 
 
 def kernel(
-    pt_hbm, occ_hbm, root_hbm, xy_hbm, kind_hbm, pot_hbm, tab, dens, ints,
-    pt, occ, root, xy, kind, pot, tables, bt, rs1, tt, pex, pout, pin, boxes, ext, rs3, st, p4, ag, isnd, ircv,
-    in_sem, tab_sem, s1, r1, s2, r2, sp, rp, s3, r3, s4, r4, s5, r5, s6, r6,
+    pt_hbm, occ_hbm, root_hbm, xy_hbm, kind_hbm, pot_hbm, tab, ag, ints_hbm,
+    pt, occ, root, xy, kind, pot, tables, bt, rs1, tt, pex, pout, pin, boxes, ext, rs3, st, p4, piece, ints, isnd, ircv,
+    in_sem, out_sem, tab_sem, s1, r1, s2, r2, sp, rp, s3, r3, s4, r4, s5, r5, s6, r6,
 ):
     me = lax.axis_index("band")
     slab = lax.axis_index("slab")
@@ -140,7 +140,7 @@
     weighted = split(p.astype(F32) * occ[...], 2)
     gram = dot_nt(weighted[0], p) + dot_nt(weighted[1], p)
     spread = jnp.zeros((size, 256), F32)
-    for part in split(jnp.where(same, gram, 0.0), 3):
+    for part in split(jnp.where(same, gram, 0.0), 2):
         spread = spread + dot(part, pick_j)
     partial = jnp.zeros((ATOMS, 256), F32)
     for i in range(NH):
@@ -305,7 +305,10 @@
         )
 
     def send5(rel):
-        return remote(ag.at[own], ag.at[own], s5.at[0], r5.at[own], band=peer(rel))
+        return remote(piece, ag.at[own], s5.at[0], r5.at[own], band=peer(rel))
+
+    def keep():
+        return pltpu.make_async_copy(piece, ag.at[own], out_sem.at[0])
 
     def start5(rel, carry):
         send5(rel).start()
@@ -367,25 +370,20 @@
         ends = [total[16:24, c * 128 : c * 128 + 128] for c in range(3)]
         ends = ends[0] + pltpu.roll(ends[1], 2, 0) + pltpu.roll(ends[2], 4, 0)
         ends = jnp.concatenate([ends, jnp.zeros_like(ends)], axis=0)
-        ag[own, :, 0:WIDE] = total[0:16].astype(BF16)
-        ag[own, :, WIDE : WIDE + 128] = ends.astype(BF16)
+        piece[:, 0:WIDE] = total[0:16].astype(BF16)
+        piece[:, WIDE : WIDE + 128] = ends.astype(BF16)
         lax.fori_loop(1, BAND, start5, 0)
+        keep().start()
 
     take(r6.at[0], ircv.at[pl.ds(0, BAND - 1)])
     ints[...] = jnp.sum(ircv[...], axis=0)
+    leave = pltpu.make_async_copy(ints, ints_hbm, out_sem.at[1])
+    leave.start()
 
     for j in range(OWNERS):
         @pl.when(me != 8 * j // 3)
         def _(j=j):
-            remote(ag.at[j], ag.at[j], s5.at[0], r5.at[j], band=8 * j // 3).wait_recv()
-
-        dens[0:16, j * WIDE : (j + 1) * WIDE] = ag[j, :, 0:WIDE]
-        ends = ag[j, :, WIDE : WIDE + 128].astype(F32)[0:8]
-        for c in range(3):
-            at = j * WIDE + c * 128
-            tail = pltpu.roll(ends, 8 - 2 * c, 0) if c else ends
-            tail = jnp.concatenate([tail, jnp.zeros_like(tail)], axis=0)
-            dens[16:32, at : at + 128] = tail.astype(BF16)
+            remote(piece, ag.at[j], s5.at[0], r5.at[j], band=8 * j // 3).wait_recv()
 
     for t in range(4):
         @pl.when(me != 4 * t)
@@ -414,10 +412,18 @@
         for k in (1, 2, 3):
             send4(k).wait_send()
         take(s5.at[0], rs3.at[pl.ds(0, BAND - 1)])
+        keep().wait()
+
+    leave.wait()
 
 
 def finish(rounded, sums, density, integrals):
-    density[...] = rounded[...].astype(F32)[0:CZ]
+    for j in range(OWNERS):
+        density[0:16, j * WIDE : (j + 1) * WIDE] = rounded[j, :, 0:WIDE].astype(F32)
+        ends = rounded[j, :, WIDE : WIDE + 128].astype(F32)
+        for c in range(3):
+            at = j * WIDE + c * 128
+            density[16:CZ, at : at + 128] = ends[2 * c : 2 * c + 2]
     integrals[...] = sums[:, 0:NPAIR]
 
 
@@ -429,11 +435,11 @@
     density, integrals = pl.pallas_call(
         kernel,
         out_shape=(
-            jax.ShapeDtypeStruct((32, GXY), BF16),
+            jax.ShapeDtypeStruct((OWNERS, 16, WIDE + 128), BF16),
             jax.ShapeDtypeStruct((1, 256), F32),
         ),
         in_specs=[pl.BlockSpec(memory_space=pltpu.HBM)] * 7,
-        out_specs=(vmem, vmem),
+        out_specs=(pl.BlockSpec(memory_space=pltpu.HBM),) * 2,
         scratch_shapes=[
             pltpu.VMEM((NH * ATOMS, 256), BF16),
             pltpu.VMEM((1, 256), F32),
@@ -453,10 +459,12 @@
             pltpu.VMEM((BAND, 16, WIDE + 128), BF16),
             pltpu.VMEM((4, WINDOW, WIDE), F32),
             pltpu.VMEM((3, WINDOW, WIDE), F32),
-            pltpu.VMEM((OWNERS, 16, WIDE + 128), BF16),
+            pltpu.VMEM((16, WIDE + 128), BF16),
+            pltpu.VMEM((1, 256), F32),
             pltpu.VMEM((ATOMS, 1, 256), F32),
             pltpu.VMEM((BAND, 1, 256), F32),
             dma((6,)),
+            dma((2,)),
             dma((DEPTH,)),
             dma((4,)), dma((1,)),
             dma((1,)), dma((4,)),

time: 47.9 us -> 47.4 us (0.990)
  Pallas kernels: 47.1 us -> 46.6 us
    pallas_call x1, Pallas kernels: 45.5 us -> 45 us  [shards(): pl.pallas_call(kernel, out_shape=(jax.ShapeDtypeStruct((OWNERS, 16, WIDE...]
where the time goes in v7:
time: 47.4 us; the launch traced here: 47.2 us
  Pallas kernels  46.6 us (98%)
  between operations  0.64 us (1%)
    pallas_call x1, Pallas kernels, shards(): pl.pallas_call(kernel, out_shape=(jax.ShapeDtypeStruct((OWNERS, 16, WIDE...  45 us
    pallas_call x1, Pallas kernels, shards(): pl.pallas_call(finish, out_shape=(jax.ShapeDtypeStruct((CZ, GXY), F32), j...  1.6 us

profile of v7, /device:TPU:1, one launch (start us, length us, event | category | flops | bytes accessed | tf_op | source)
XLA Modules:
  0.0 47.2 jit_solution(15083158982430532616)
XLA Ops:
  0.6 45.0 %shard_map.86 = (bf16[6,16,512]{2,1,0:T(8,128)(2,1)}, f32[1,256]{1,0:T(1,128)}) custom-call(bf16[288,256]{1,0:T(8,128)(2,1)} %bitcast.12, f32[1,256]{1,0:T(1,128)} %bitcast.13, s32[1,16]{1,0:T(1,128)} %bitcast.14, s32[1,16]{1,0:T(1,128)} %bitcast.15, s32[1,16]{1,0:T(1,128)} %bitcast.16, f32[18,2304]{1,0:T(8,128)} %pot_hbm.1, ...), custom_call_target="tpu_custom_call" | custom-call | tf_op jit(solution)/shard_map/pallas_call | solution.py:435
  45.6 1.6 %shard_map.87 = (f32[18,2304]{1,0:T(8,128)}, f32[1,171]{1,0:T(1,128)}) custom-call(bf16[6,16,512]{2,1,0:T(8,128)(2,1)} %get-tuple-element.6.rounded, f32[1,256]{1,0:T(1,128)} %get-tuple-element.7.sums), custom_call_target="tpu_custom_call" | custom-call | tf_op jit(solution)/shard_map/pallas_call | solution.py:489
